TPU v7x, 32 devices: a whole 2x2x4 slice. The times are simulated.
32 devices in a mesh: dp: 2 (over core), wide: 16 (over z, y, x).
Axes of the slice: x: 2, y: 2, z: 4, core: 2. Of those that a mesh axis runs over, the one named last changes fastest.
Arguments:
- tokens: bfloat16 [32, 1024, 256], P(('dp', 'wide')), may hold values from -6 to 6
- item_lengths: int32 [32, 20], P(('dp', 'wide')), may hold values from 5 to 100, as said below
- loop_counts: int32 [32, 20], P(('dp', 'wide')), may hold values from 1 to 2
- w_query: bfloat16 [256, 256], P('wide'), may hold values from -0.5 to 0.5
- w_key: bfloat16 [256, 256], P('wide'), may hold values from -0.5 to 0.5
- w_value: bfloat16 [256, 256], P('wide'), may hold values from -0.375 to 0.375
- w_out: bfloat16 [256, 256], P(None, 'wide'), may hold values from -1.5 to 1.5
- w_up: bfloat16 [256, 1024], P('wide'), may hold values from -0.375 to 0.375
- w_down: bfloat16 [1024, 256], P(None, 'wide'), may hold values from -0.1875 to 0.1875
- gain_one: bfloat16 [256], P('wide'), may hold values from 0.25 to 1.75
- shift_one: bfloat16 [256], P('wide'), may hold values from -4 to 4
- gain_two: bfloat16 [256], P('wide'), may hold values from 0.25 to 1.75
- shift_two: bfloat16 [256], P('wide'), may hold values from -4 to 4
- bias_up: bfloat16 [1024], P('wide'), may hold values from -4 to 4
- bias_down: bfloat16 [256], P('wide'), may hold values from -4 to 4
- cotangent: bfloat16 [32, 1024, 256], P(('dp', 'wide')), may hold values from -6 to 6
Outputs:
- output: bfloat16 [32, 1024, 256], P(('dp', 'wide'))
- input_grad: bfloat16 [32, 1024, 256], P(('dp', 'wide'))
- grad_query: float32 [256, 256], P('wide')
- grad_key: float32 [256, 256], P('wide')
- grad_value: float32 [256, 256], P('wide')
- grad_out: float32 [256, 256], P(None, 'wide')
- grad_up: float32 [256, 1024], P('wide')
- grad_down: float32 [1024, 256], P(None, 'wide')
- grad_gain_one: float32 [256], P('wide')
- grad_shift_one: float32 [256], P('wide')
- grad_gain_two: float32 [256], P('wide')
- grad_shift_two: float32 [256], P('wide')
- grad_bias_up: float32 [1024], P('wide')
- grad_bias_down: float32 [256], P('wide')
Inputs may be any that keep to these rules, and one draw needn't show every extreme that they name: `item_lengths`: in each row the 20 item lengths add up to 1024; each row has at least one item of exactly 100 slots and at least one of exactly 5.
All inputs are finite; a program needn't handle non-finite values.
Results may differ from a plain program's by a relative error of at most 0.017.
The roundings to bfloat16 on the way count: a program that leaves them out, or rounds other values in their place, can miss the bound.
Values may be sent and summed in bfloat16 or wider, within the bound.
A program may use at most 192 MiB of HBM per device.

v0:
```python
import jax
import jax.numpy as jnp
from jax import lax
from jax.sharding import PartitionSpec as P

HEADS = 4
LOOPS = 2


NORM_EPS = 1e-05
MASK_FILL = -1e30


def split_up(shard, dim, devices):
    dims = shard.shape
    blocks = shard.reshape(*dims[:dim], devices, dims[dim] // devices, *dims[dim + 1 :])
    return jnp.moveaxis(blocks, dim, 0)


def summed_on_arrival(shard, axis, dim):
    devices = lax.axis_size(axis)
    blocks = lax.all_to_all(split_up(shard, dim, devices), axis, 0, 0, tiled=True)
    return jnp.sum(blocks.astype(jnp.float32), axis=0)


def sent_together(arrays, axis, dim, along):
    ends, at = ([], 0)
    for a in arrays[:-1]:
        at += a.shape[along]
        ends.append(at)
    both = jnp.concatenate(arrays, axis=along)
    return tuple(jnp.split(summed_on_arrival(both, axis, dim), ends, axis=along))


def layer_norm(values, norm_gain, norm_shift):
    average = jnp.mean(values, axis=-1, keepdims=True)
    centered = values - average
    spread = jnp.mean(centered * centered, axis=-1, keepdims=True)
    return centered * lax.rsqrt(spread + NORM_EPS) * norm_gain + norm_shift


def gelu_tanh(values):
    return jax.nn.gelu(values, approximate=True)


def row_layout(lengths, counts, slot_count):
    item_ends = jnp.cumsum(lengths)
    positions = jnp.arange(slot_count, dtype=jnp.int32)
    item_of = jnp.sum((item_ends[None, :] <= positions[:, None]).astype(jnp.int32), axis=1)
    matches = item_of[:, None] == jnp.arange(lengths.shape[0], dtype=jnp.int32)[None, :]
    loops_slot = jnp.sum(jnp.where(matches, counts[None, :], 0), axis=1)
    allowed = (item_of[:, None] == item_of[None, :]) & (positions[None, :] <= positions[:, None])
    return (loops_slot, allowed)


def block_parts(current, inputs, allowed, params):
    (
        w_query,
        w_key,
        w_value,
        w_out,
        w_up,
        w_down,
        gain_one,
        shift_one,
        gain_two,
        shift_two,
        bias_up,
        bias_down,
    ) = params
    slot_count, width = current.shape
    head_dim = width // HEADS
    scaling = head_dim ** (-0.5)
    mixed_in = current + inputs
    normed = layer_norm(mixed_in, gain_one, shift_one).astype(jnp.bfloat16)
    queries = (
        jnp.dot(normed, w_query, preferred_element_type=jnp.float32)
        .astype(jnp.bfloat16)
        .reshape(slot_count, HEADS, head_dim)
    )
    keys_act = (
        jnp.dot(normed, w_key, preferred_element_type=jnp.float32)
        .astype(jnp.bfloat16)
        .reshape(slot_count, HEADS, head_dim)
    )
    values_act = (
        jnp.dot(normed, w_value, preferred_element_type=jnp.float32)
        .astype(jnp.bfloat16)
        .reshape(slot_count, HEADS, head_dim)
    )
    scores = (
        jnp.einsum("qhd,khd->hqk", queries, keys_act, preferred_element_type=jnp.float32) * scaling
    )
    scores = jnp.where(allowed[None, :, :], scores, MASK_FILL)
    largest = jnp.max(scores, axis=-1, keepdims=True)
    exponent = jnp.exp(scores - largest)
    attn_probs = exponent / jnp.sum(exponent, axis=-1, keepdims=True)
    probs_low = attn_probs.astype(jnp.bfloat16)
    attended = jnp.einsum("hqk,khd->qhd", probs_low, values_act, preferred_element_type=jnp.float32)
    attended = attended.reshape(slot_count, width).astype(jnp.bfloat16)
    residual = mixed_in + jnp.dot(attended, w_out, preferred_element_type=jnp.float32)
    normed_two = layer_norm(residual, gain_two, shift_two).astype(jnp.bfloat16)
    hidden_pre = jnp.dot(normed_two, w_up, preferred_element_type=jnp.float32) + bias_up
    hidden_act = gelu_tanh(hidden_pre).astype(jnp.bfloat16)
    renewed = residual + jnp.dot(hidden_act, w_down, preferred_element_type=jnp.float32) + bias_down
    return (
        mixed_in,
        normed,
        queries,
        keys_act,
        values_act,
        attn_probs,
        probs_low,
        attended,
        residual,
        normed_two,
        hidden_pre,
        hidden_act,
        renewed,
    )


def block_backward(current, inputs, allowed, params, back_renewed):
    (
        w_query,
        w_key,
        w_value,
        w_out,
        w_up,
        w_down,
        gain_one,
        shift_one,
        gain_two,
        shift_two,
        bias_up,
        bias_down,
    ) = params
    (
        mixed_in,
        normed,
        queries,
        keys_act,
        values_act,
        attn_probs,
        probs_low,
        attended,
        residual,
        normed_two,
        hidden_pre,
        hidden_act,
        renewed,
    ) = block_parts(current, inputs, allowed, params)
    slot_count, width = current.shape
    head_dim = width // HEADS
    scaling = head_dim ** (-0.5)
    back_two = back_renewed.astype(jnp.bfloat16)
    grad_down = jnp.einsum("sf,sd->fd", hidden_act, back_two, preferred_element_type=jnp.float32)
    grad_bias_down = jnp.sum(back_two.astype(jnp.float32), axis=0)
    back_hidden = jnp.einsum("sd,fd->sf", back_two, w_down, preferred_element_type=jnp.float32)
    gelu_pull = jax.vjp(gelu_tanh, hidden_pre)[1]
    back_pre = gelu_pull(back_hidden)[0].astype(jnp.bfloat16)
    grad_up = jnp.einsum("sd,sf->df", normed_two, back_pre, preferred_element_type=jnp.float32)
    grad_bias_up = jnp.sum(back_pre.astype(jnp.float32), axis=0)
    back_normtwo = jnp.einsum("sf,df->sd", back_pre, w_up, preferred_element_type=jnp.float32)
    norm_pull_two = jax.vjp(layer_norm, residual, gain_two, shift_two)[1]
    back_res_norm, grad_gain_two, grad_shift_two = norm_pull_two(back_normtwo)
    back_resid = back_renewed + back_res_norm
    back_one = back_resid.astype(jnp.bfloat16)
    grad_out = jnp.einsum("sd,se->de", attended, back_one, preferred_element_type=jnp.float32)
    back_attend = jnp.einsum("se,de->sd", back_one, w_out, preferred_element_type=jnp.float32)
    back_attend = back_attend.astype(jnp.bfloat16).reshape(slot_count, HEADS, head_dim)
    back_values = jnp.einsum(
        "hqk,qhd->khd", probs_low, back_attend, preferred_element_type=jnp.float32
    )
    back_values = back_values.reshape(slot_count, width).astype(jnp.bfloat16)
    back_probs = jnp.einsum(
        "qhd,khd->hqk", back_attend, values_act, preferred_element_type=jnp.float32
    )
    back_scores = attn_probs * (
        back_probs - jnp.sum(back_probs * attn_probs, axis=-1, keepdims=True)
    )
    back_scores = back_scores.astype(jnp.bfloat16)
    back_queries = (
        jnp.einsum("hqk,khd->qhd", back_scores, keys_act, preferred_element_type=jnp.float32)
        * scaling
    )
    back_queries = back_queries.reshape(slot_count, width).astype(jnp.bfloat16)
    back_keys = (
        jnp.einsum("hqk,qhd->khd", back_scores, queries, preferred_element_type=jnp.float32)
        * scaling
    )
    back_keys = back_keys.reshape(slot_count, width).astype(jnp.bfloat16)
    grad_query = jnp.einsum("sd,se->de", normed, back_queries, preferred_element_type=jnp.float32)
    grad_key = jnp.einsum("sd,se->de", normed, back_keys, preferred_element_type=jnp.float32)
    grad_value = jnp.einsum("sd,se->de", normed, back_values, preferred_element_type=jnp.float32)
    back_normed = jnp.einsum("se,de->sd", back_queries, w_query, preferred_element_type=jnp.float32)
    back_normed = back_normed + jnp.einsum(
        "se,de->sd", back_keys, w_key, preferred_element_type=jnp.float32
    )
    back_normed = back_normed + jnp.einsum(
        "se,de->sd", back_values, w_value, preferred_element_type=jnp.float32
    )
    norm_pull_one = jax.vjp(layer_norm, mixed_in, gain_one, shift_one)[1]
    back_mix_norm, grad_gain_one, grad_shift_one = norm_pull_one(back_normed)
    back_mixed = back_resid + back_mix_norm
    grads_here = (
        grad_query,
        grad_key,
        grad_value,
        grad_out,
        grad_up,
        grad_down,
        grad_gain_one,
        grad_shift_one,
        grad_gain_two,
        grad_shift_two,
        grad_bias_up,
        grad_bias_down,
    )
    return (back_mixed, grads_here)


def on_device(
    tokens,
    item_lengths,
    loop_counts,
    w_query,
    w_key,
    w_value,
    w_out,
    w_up,
    w_down,
    gain_one,
    shift_one,
    gain_two,
    shift_two,
    bias_up,
    bias_down,
    cotangent,
):
    gathered = (
        lax.all_gather(w_query, "wide", axis=0, tiled=True),
        lax.all_gather(w_key, "wide", axis=0, tiled=True),
        lax.all_gather(w_value, "wide", axis=0, tiled=True),
        lax.all_gather(w_out, "wide", axis=1, tiled=True),
        lax.all_gather(w_up, "wide", axis=0, tiled=True),
        lax.all_gather(w_down, "wide", axis=1, tiled=True),
        lax.all_gather(gain_one, "wide", axis=0, tiled=True),
        lax.all_gather(shift_one, "wide", axis=0, tiled=True),
        lax.all_gather(gain_two, "wide", axis=0, tiled=True),
        lax.all_gather(shift_two, "wide", axis=0, tiled=True),
        lax.all_gather(bias_up, "wide", axis=0, tiled=True),
        lax.all_gather(bias_down, "wide", axis=0, tiled=True),
    )
    params = tuple(
        (
            gathered_one if gathered_one.ndim == 2 else gathered_one.astype(jnp.float32)
            for gathered_one in gathered
        )
    )
    zero_grads = tuple((jnp.zeros(param_one.shape, jnp.float32) for param_one in params))

    def row_step(totals, packed):
        inputs_low, lengths, counts, upstream = packed
        loops_slot, allowed = row_layout(lengths, counts, inputs_low.shape[0])
        inputs = inputs_low.astype(jnp.float32)
        loop_inputs = [inputs]
        current = inputs
        for loop_turn in range(LOOPS):
            renewed = block_parts(current, inputs, allowed, params)[-1]
            current = jnp.where((loops_slot > loop_turn)[:, None], renewed, current)
            loop_inputs.append(current)
        back_state = upstream.astype(jnp.float32)
        back_input = jnp.zeros_like(inputs)
        for loop_turn in reversed(range(LOOPS)):
            active = (loops_slot > loop_turn)[:, None]
            back_mixed, grads_here = block_backward(
                loop_inputs[loop_turn], inputs, allowed, params, jnp.where(active, back_state, 0.0)
            )
            totals = tuple((running + addend for running, addend in zip(totals, grads_here)))
            back_input = back_input + back_mixed
            back_state = jnp.where(active, 0.0, back_state) + back_mixed
        return (
            totals,
            (current.astype(jnp.bfloat16), (back_input + back_state).astype(jnp.bfloat16)),
        )

    totals, (output, input_grad) = lax.scan(
        row_step, zero_grads, (tokens, item_lengths, loop_counts, cotangent)
    )
    (
        total_query,
        total_key,
        total_value,
        total_out,
        total_up,
        total_down,
        total_gain_one,
        total_shift_one,
        total_gain_two,
        total_shift_two,
        total_bias_up,
        total_bias_down,
    ) = totals
    scattered = (
        *sent_together(
            (
                total_query.astype(jnp.bfloat16),
                total_key.astype(jnp.bfloat16),
                total_value.astype(jnp.bfloat16),
            ),
            "wide",
            0,
            1,
        ),
        summed_on_arrival(total_out.astype(jnp.bfloat16), "wide", 1),
        summed_on_arrival(total_up.astype(jnp.bfloat16), "wide", 0),
        summed_on_arrival(total_down.astype(jnp.bfloat16), "wide", 1),
        summed_on_arrival(total_gain_one.astype(jnp.bfloat16), "wide", 0),
        summed_on_arrival(total_shift_one.astype(jnp.bfloat16), "wide", 0),
        summed_on_arrival(total_gain_two.astype(jnp.bfloat16), "wide", 0),
        summed_on_arrival(total_shift_two.astype(jnp.bfloat16), "wide", 0),
        summed_on_arrival(total_bias_up.astype(jnp.bfloat16), "wide", 0),
        summed_on_arrival(total_bias_down.astype(jnp.bfloat16), "wide", 0),
    )
    (
        part_query,
        part_key,
        part_value,
        part_out,
        part_up,
        part_down,
        part_gain_one,
        part_shift_one,
        part_gain_two,
        part_shift_two,
        part_bias_up,
        part_bias_down,
    ) = scattered
    owned = (
        lax.psum(part_query.astype(jnp.bfloat16), "dp").astype(jnp.float32),
        lax.psum(part_key.astype(jnp.bfloat16), "dp").astype(jnp.float32),
        lax.psum(part_value.astype(jnp.bfloat16), "dp").astype(jnp.float32),
        lax.psum(part_out.astype(jnp.bfloat16), "dp").astype(jnp.float32),
        lax.psum(part_up.astype(jnp.bfloat16), "dp").astype(jnp.float32),
        lax.psum(part_down.astype(jnp.bfloat16), "dp").astype(jnp.float32),
        lax.psum(part_gain_one.astype(jnp.bfloat16), "dp").astype(jnp.float32),
        lax.psum(part_shift_one.astype(jnp.bfloat16), "dp").astype(jnp.float32),
        lax.psum(part_gain_two.astype(jnp.bfloat16), "dp").astype(jnp.float32),
        lax.psum(part_shift_two.astype(jnp.bfloat16), "dp").astype(jnp.float32),
        lax.psum(part_bias_up.astype(jnp.bfloat16), "dp").astype(jnp.float32),
        lax.psum(part_bias_down.astype(jnp.bfloat16), "dp").astype(jnp.float32),
    )
    return (
        output,
        input_grad,
        owned[0],
        owned[1],
        owned[2],
        owned[3],
        owned[4],
        owned[5],
        owned[6],
        owned[7],
        owned[8],
        owned[9],
        owned[10],
        owned[11],
    )


def solution(mesh):
    in_specs = (
        P(("dp", "wide"), None, None),
        P(("dp", "wide"), None),
        P(("dp", "wide"), None),
        P("wide", None),
        P("wide", None),
        P("wide", None),
        P(None, "wide"),
        P("wide", None),
        P(None, "wide"),
        P("wide"),
        P("wide"),
        P("wide"),
        P("wide"),
        P("wide"),
        P("wide"),
        P(("dp", "wide"), None, None),
    )
    out_specs = (
        P(("dp", "wide"), None, None),
        P(("dp", "wide"), None, None),
        P("wide", None),
        P("wide", None),
        P("wide", None),
        P(None, "wide"),
        P("wide", None),
        P(None, "wide"),
        P("wide"),
        P("wide"),
        P("wide"),
        P("wide"),
        P("wide"),
        P("wide"),
    )
    return jax.shard_map(
        on_device, mesh=mesh, in_specs=in_specs, out_specs=out_specs, check_vma=False
    )
```

profile of v0, /device:TPU:0, one launch (start us, length us, event | category | flops | bytes accessed | tf_op | source)
XLA Modules:
  0.0 638.2 jit_solution(5426992690135873247)
XLA Ops:
  14.8 44.0 %all-reduce.6 = (bf16[256]{0:T(256)(128)(2,1)S(1)}, bf16[256]{0:T(256)(128)(2,1)S(1)}, bf16[256]{0:T(256)(128)(2,1)S(1)}, bf16[256]{0:T(256)(128)(2,1)S(1)}, bf1...) all-reduce(bf16[256]{0:T(256)(128)(2,1)S(1)} %dynamic-update-slice.1, ...), channel_id=1, replica_groups=mesh['dp'=2,'wide'=16] {'wide'}, use_global_device_ids=true, to_apply=%add.1 | all-reduce | flops 2304 | bytes 9216
  63.6 36.4 %all_gather.39 = bf16[256,256]{1,0:T(8,128)(2,1)S(1)} all-gather(bf16[16,256]{1,0:T(8,128)(2,1)} %param.19), channel_id=1, replica_groups=mesh['dp'=2,'wide'=16] {'wide'}, dimensions={0}, use_global_device_ids=true | all-gather | bytes 139264 | tf_op jit(solution)/shard_map/all_gather | solution.py:242
  100.1 38.3 %all_gather.40 = bf16[256,256]{1,0:T(8,128)(2,1)S(1)} all-gather(bf16[16,256]{1,0:T(8,128)(2,1)} %param.20), channel_id=1, replica_groups=mesh['dp'=2,'wide'=16] {'wide'}, dimensions={0}, use_global_device_ids=true | all-gather | bytes 139264 | tf_op jit(solution)/shard_map/all_gather | solution.py:243
  138.4 36.4 %all_gather.38 = bf16[256,256]{1,0:T(8,128)(2,1)S(1)} all-gather(bf16[16,256]{1,0:T(8,128)(2,1)} %param.21), channel_id=1, replica_groups=mesh['dp'=2,'wide'=16] {'wide'}, dimensions={0}, use_global_device_ids=true | all-gather | bytes 139264 | tf_op jit(solution)/shard_map/all_gather | solution.py:244
  174.9 38.5 %all_gather.41 = bf16[256,256]{0,1:T(8,128)(2,1)S(1)} all-gather(bf16[256,16]{0,1:T(8,128)(2,1)} %param.22), channel_id=1, replica_groups=mesh['dp'=2,'wide'=16] {'wide'}, dimensions={1}, use_global_device_ids=true | all-gather | bytes 139264 | tf_op jit(solution)/shard_map/all_gather | solution.py:245
  215.0 38.7 %all_gather.44 = bf16[256,1024]{1,0:T(8,128)(2,1)S(1)} all-gather(bf16[16,1024]{1,0:T(8,128)(2,1)} %param.23), channel_id=1, replica_groups=mesh['dp'=2,'wide'=16] {'wide'}, dimensions={0}, use_global_device_ids=true | all-gather | bytes 557056 | tf_op jit(solution)/shard_map/all_gather | solution.py:246
  253.7 42.4 %all_gather.46 = bf16[1024,256]{0,1:T(8,128)(2,1)} all-gather(bf16[1024,16]{0,1:T(8,128)(2,1)S(1)} %copy-done.74), channel_id=1, replica_groups=mesh['dp'=2,'wide'=16] {'wide'}, dimensions={1}, use_global_device_ids=true | all-gather | bytes 557056 | tf_op jit(solution)/shard_map/all_gather | solution.py:247
  299.2 11.1 %fusion.123 = (f32[4,1024]{1,0:T(4,128)S(1)}, f32[4,1024,1024]{1,2,0:T(8,128)}) fusion(pred[1024,1024]{0,1:T(8,128)(4,1)S(1)} %fusion.32, bf16[1024,4,64]{0,2,1:T(8,128)(2,1)} %bitcast.218, bf16[1024,4,64]{0,2,1:T(8,128)(2,1)S(1)} %bitcast.216), kind=kOutput, calls=%fused_computation.204 | convolution fusion | flops 553649152 | bytes 18890752 | tf_op jit(solution)/shard_map/while/body/eval_jaxpr/sub | solution.py:96
  310.3 7.5 %fusion.49 = bf16[4,64,1024]{2,1,0:T(8,128)(2,1)S(1)} fusion(bf16[1024,4,64]{0,2,1:T(8,128)(2,1)} %bitcast.232, f32[4,1024,1024]{1,2,0:T(8,128)} %get-tuple-element.209, f32[4,1024]{1,0:T(4,128)S(1)} %get-tuple-element.208), kind=kOutput, calls=%fused_computation.88 | convolution fusion | flops 545521664 | bytes 17842176 | tf_op jit(solution)/shard_map/while/body/eval_jaxpr/hqk,khd->qhd/dot_general | solution.py:99
  319.4 2.7 fusion.120
  325.8 2.0 copy.115
  327.9 11.9 %fusion.125 = (f32[4,1024]{1,0:T(4,128)}, f32[4,1024,1024]{1,2,0:T(8,128)}) fusion(pred[1024,1024]{0,1:T(8,128)(4,1)} %copy-done.33, bf16[1024,4,64]{0,2,1:T(8,128)(2,1)} %bitcast.205, bf16[1024,4,64]{0,2,1:T(8,128)(2,1)S(1)} %bitcast.203), kind=kOutput, calls=%fused_computation.206 | convolution fusion | flops 553649152 | bytes 18890752 | tf_op jit(solution)/shard_map/while/body/eval_jaxpr/sub | solution.py:96
  339.8 7.4 %fusion.55 = bf16[4,64,1024]{2,1,0:T(8,128)(2,1)S(1)} fusion(bf16[1024,4,64]{0,2,1:T(8,128)(2,1)} %bitcast.221, f32[4,1024,1024]{1,2,0:T(8,128)} %get-tuple-element.214, f32[4,1024]{1,0:T(4,128)} %get-tuple-element.213), kind=kOutput, calls=%fused_computation.90 | convolution fusion | flops 545521664 | bytes 17842176 | tf_op jit(solution)/shard_map/while/body/eval_jaxpr/hqk,khd->qhd/dot_general | solution.py:99
  349.9 4.1 convert_reduce_fusion.1
  354.0 2.3 fusion.127
  356.3 2.6 copy.116
  358.9 2.1 multiply_reduce_fusion.3
  363.8 8.5 %fusion.58 = bf16[4,64,1024]{2,1,0:T(8,128)(2,1)S(1)} fusion(bf16[1024,4,64]{0,2,1:T(8,128)(2,1)S(1)} %bitcast.226, f32[4,1024,1024]{1,2,0:T(8,128)} %get-tuple-element.214, f32[4,1024]{1,0:T(4,128)S(1)} %copy-done.85), kind=kOutput, calls=%fused_computation.91 | convolution fusion | flops 545521664 | bytes 17842176 | tf_op jit(solution)/shard_map/while/body/eval_jaxpr/hqk,qhd->khd/dot_general | solution.py:172
  372.3 10.7 %multiply_reduce_fusion.1 = (f32[4,1024]{1,0:T(4,128)S(1)}, f32[4,1024,1024]{1,2,0:T(8,128)}) fusion(f32[4,1024,1024]{1,2,0:T(8,128)} %get-tuple-element.214, f32[4,1024]{1,0:T(4,128)S(1)} %copy-done.85, bf16[1024,4,64]{0,2,1:T(8,128)(2,1)S(1)} %bitcast.227, bf16[1024,4,64]{0,2,1:T(8,128)(2,1)S(1)} %bitcast.222), kind=kOutput, calls=%fused_computation.5 | convolution fusion | flops 549449728 | bytes 34635776 | tf_op jit(solution)/shard_map/while/body/eval_jaxpr/qhd,khd->hqk/dot_general | solution.py:176
  383.0 11.9 %multiply_convert_fusion.1 = bf16[4,1024,1024]{1,2,0:T(8,128)(2,1)S(1)} fusion(f32[4,1024,1024]{1,2,0:T(8,128)} %get-tuple-element.218, f32[4,1024]{1,0:T(4,128)S(1)} %get-tuple-element.217, f32[4,1024,1024]{1,2,0:T(8,128)} %get-tuple-element.214, f32[4,1024]{1,0:T(4,128)S(1)} %copy-done.85), kind=kLoop, calls=%fused_computation.4 | loop fusion | flops 16777216 | bytes 41975808 | tf_op jit(solution)/shard_map/while/body/eval_jaxpr/convert_element_type | solution.py:182
  394.9 2.7 fusion.65
  397.6 1.6 fusion.64
  402.1 1.8 convert_reduce_fusion.2
  404.7 4.1 all-to-all-start.9
  408.8 2.2 fusion.132
  411.0 2.3 fusion.131
  413.3 2.2 fusion.129
  415.5 6.5 %convert_reduce_fusion = (f32[1024]{0:T(1024)}, bf16[1024,1024]{1,0:T(8,128)(2,1)S(1)}) fusion(f32[1024,1024]{1,0:T(8,128)} %copy-done.19, f32[1024]{0:T(1024)} %convert_element_type.448, bf16[1024,256]{0,1:T(8,128)(2,1)} %get-tuple-element.194, bf16[1024,256]{0,1:T(8,128)(2,1)} %all_gather.46), kind=kOutput, calls=%fused_computation.38 | convolution fusion | flops 560987136 | bytes 7348224 | tf_op jit(solution)/shard_map/while/body/eval_jaxpr/sd,fd->sf/dot_general | solution.py:159
  422.0 2.3 fusion.128
  424.3 2.6 copy.123
  427.0 2.2 multiply_reduce_fusion.2
  429.2 1.5 fusion.118
  432.1 8.5 %fusion.52 = bf16[4,64,1024]{2,1,0:T(8,128)(2,1)S(1)} fusion(bf16[1024,4,64]{0,2,1:T(8,128)(2,1)S(1)} %bitcast.224, f32[4,1024,1024]{1,2,0:T(8,128)} %get-tuple-element.209, f32[4,1024]{1,0:T(4,128)S(1)} %copy-done.84), kind=kOutput, calls=%fused_computation.89 | convolution fusion | flops 545521664 | bytes 17842176 | tf_op jit(solution)/shard_map/while/body/eval_jaxpr/hqk,qhd->khd/dot_general | solution.py:172
  440.6 10.5 %multiply_reduce_fusion = (f32[4,1024]{1,0:T(4,128)S(1)}, f32[4,1024,1024]{1,2,0:T(8,128)}) fusion(f32[4,1024,1024]{1,2,0:T(8,128)} %get-tuple-element.209, f32[4,1024]{1,0:T(4,128)S(1)} %copy-done.84, bf16[1024,4,64]{0,2,1:T(8,128)(2,1)S(1)} %bitcast.225, bf16[1024,4,64]{0,2,1:T(8,128)(2,1)S(1)} %bitcast.233), kind=kOutput, calls=%fused_computation.3 | convolution fusion | flops 549449728 | bytes 34635776 | tf_op jit(solution)/shard_map/while/body/eval_jaxpr/qhd,khd->hqk/dot_general | solution.py:176
  451.1 11.9 %multiply_convert_fusion = bf16[4,1024,1024]{1,2,0:T(8,128)(2,1)S(1)} fusion(f32[4,1024,1024]{1,2,0:T(8,128)} %get-tuple-element.221, f32[4,1024]{1,0:T(4,128)S(1)} %get-tuple-element.220, f32[4,1024,1024]{1,2,0:T(8,128)} %get-tuple-element.209, f32[4,1024]{1,0:T(4,128)S(1)} %copy-done.84), kind=kLoop, calls=%fused_computation.2 | loop fusion | flops 16777216 | bytes 41975808 | tf_op jit(solution)/shard_map/while/body/eval_jaxpr/convert_element_type | solution.py:182
  463.0 2.7 fusion.67
  465.8 1.6 fusion.66
  474.7 6.8 %all-to-all-start.7 = ((bf16[16,1,16]{2,1,0:T(2,128)(2,1)}), bf16[16,1,16]{2,1,0:T(2,128)(2,1)S(1)}, u32[]{:S(2)}, u32[]{:S(2)}) async-start(bf16[16,1,16]{2,1,0:T(2,128)(2,1)} %convert_element_type.536), calls=%async_computation.7 | async-start | bytes 16384 | tf_op jit(solution)/shard_map/all_to_all | solution.py:22
  482.2 6.5 %all-to-all-done.7 = bf16[16,1,16]{2,1,0:T(2,128)(2,1)S(1)} async-done(((bf16[16,1,16]{2,1,0:T(2,128)(2,1)}), bf16[16,1,16]{2,1,0:T(2,128)(2,1)S(1)}, u32[]{:S(2)}, u32[]{:S(2)}) %all-to-all-start.7) | async-done | bytes 544 | tf_op jit(solution)/shard_map/all_to_all | solution.py:22
  488.7 3.5 all-to-all-start.6
  492.9 6.5 %all-to-all-done.6 = bf16[16,1,16]{2,1,0:T(2,128)(2,1)S(1)} async-done(((bf16[16,1,16]{2,1,0:T(2,128)(2,1)}), bf16[16,1,16]{2,1,0:T(2,128)(2,1)S(1)}, u32[]{:S(2)}, u32[]{:S(2)}) %all-to-all-start.6) | async-done | bytes 544 | tf_op jit(solution)/shard_map/all_to_all | solution.py:22
  499.3 3.5 all-to-all-start.5
  503.5 6.6 %all-to-all-done.5 = bf16[16,1,16]{2,1,0:T(2,128)(2,1)S(1)} async-done(((bf16[16,1,16]{2,1,0:T(2,128)(2,1)}), bf16[16,1,16]{2,1,0:T(2,128)(2,1)S(1)}, u32[]{:S(2)}, u32[]{:S(2)}) %all-to-all-start.5) | async-done | bytes 544 | tf_op jit(solution)/shard_map/all_to_all | solution.py:22
  510.1 3.5 all-to-all-start.4
  514.3 6.5 %all-to-all-done.4 = bf16[16,1,16]{2,1,0:T(2,128)(2,1)S(1)} async-done(((bf16[16,1,16]{2,1,0:T(2,128)(2,1)}), bf16[16,1,16]{2,1,0:T(2,128)(2,1)S(1)}, u32[]{:S(2)}, u32[]{:S(2)}) %all-to-all-start.4) | async-done | bytes 544 | tf_op jit(solution)/shard_map/all_to_all | solution.py:22
  520.7 3.5 all-to-all-start.8
  525.6 5.8 all-to-all-done.8
  531.4 4.2 all-to-all-start.1
  539.1 4.3 all-to-all-done.1
  543.4 3.6 all-to-all-start
  547.0 4.1 fusion.92
  551.1 2.6 fusion.63
  553.7 2.8 all-to-all-done
  556.5 4.5 all-to-all-start.3
  561.1 2.5 fusion.108
  563.6 1.6 fusion.62
  565.2 6.6 %all-to-all-done.3 = bf16[16,1024,16]{1,2,0:T(8,128)(2,1)} async-done(((bf16[16,1024,16]{1,2,0:T(8,128)(2,1)}), bf16[16,1024,16]{1,2,0:T(8,128)(2,1)}, u32[]{:S(2)}, u32[]{:S(2)}) %all-to-all-start.3) | async-done | bytes 524320 | tf_op jit(solution)/shard_map/all_to_all | solution.py:22
  571.8 4.2 all-to-all-start.2
  576.7 5.2 fusion.70
  589.4 1.5 reduce_sum.632
  591.6 1.7 reduce_sum.634
  593.4 1.7 reduce_sum.633
  595.2 2.3 fusion.91
  599.5 16.6 %all-reduce.10.cloned.1.call-done = (bf16[16,256]{1,0:T(8,128)(2,1)}, bf16[16,256]{1,0:T(8,128)(2,1)}, bf16[16,256]{1,0:T(8,128)(2,1)}, bf16[256,16]{0,1:T(8,128...) async-done(((bf16[16,256]{1,0:T(8,128)(2,1)}, ...) | async-done | bytes 98608 | tf_op jit(solution)/shard_map/psum | solution.py:341
  (343 shorter events, 71.2 us)
Async XLA Ops:
  7.2 246.5 %copy-start.74 = (bf16[1024,16]{0,1:T(8,128)(2,1)S(1)}, bf16[1024,16]{0,1:T(8,128)(2,1)}, u32[]{:S(2)}) copy-start(bf16[1024,16]{0,1:T(8,128)(2,1)} %param.24) | copy-start | bytes 98308
  58.9 239.1 %copy-start.102 = (f32[256]{0:T(256)}, f32[256]{0:T(256)S(1)}, u32[]{:S(2)}) copy-start(f32[256]{0:T(256)S(1)} %convert_element_type.436) | copy-start | bytes 3076
  58.9 239.0 %copy-start.50 = (f32[256]{0:T(256)}, f32[256]{0:T(256)S(1)}, u32[]{:S(2)}) copy-start(f32[256]{0:T(256)S(1)} %convert_element_type.435) | copy-start | bytes 3076
  58.9 259.5 %copy-start.70 = (f32[256]{0:T(256)}, f32[256]{0:T(256)S(1)}, u32[]{:S(2)}) copy-start(f32[256]{0:T(256)S(1)} %convert_element_type.445) | copy-start | bytes 3076
  62.3 236.9 %copy-start.33 = (pred[1024,1024]{0,1:T(8,128)(4,1)}, pred[1024,1024]{0,1:T(8,128)(4,1)S(1)}, u32[]{:S(2)}) copy-start(pred[1024,1024]{0,1:T(8,128)(4,1)S(1)} %fusion.32) | copy-start | bytes 3145732
  138.4 160.8 %copy-start.29 = (bf16[256,256]{1,0:T(8,128)(2,1)}, bf16[256,256]{1,0:T(8,128)(2,1)S(1)}, u32[]{:S(2)}) copy-start(bf16[256,256]{1,0:T(8,128)(2,1)S(1)} %all_gather.40) | copy-start | bytes 393220
  214.6 104.7 %copy-start.2 = (bf16[1,1024,256]{1,2,0:T(8,128)(2,1)}, bf16[1,1024,256]{1,2,0:T(8,128)(2,1)S(1)}, u32[]{:S(2)}) copy-start(bf16[1,1024,256]{1,2,0:T(8,128)(2,1)S(1)} %copy.111) | copy-start | bytes 1572868
  214.8 95.5 %copy-start.45 = (f32[1024]{0:T(1024)}, f32[1024]{0:T(1024)S(1)}, u32[]{:S(2)}) copy-start(f32[1024]{0:T(1024)S(1)} %broadcast_multiply_fusion.3) | copy-start | bytes 12292
  215.0 95.3 %copy-start.56 = (f32[1024]{0:T(1024)}, f32[1024]{0:T(1024)S(1)}, u32[]{:S(2)}) copy-start(f32[1024]{0:T(1024)S(1)} %fusion.80) | copy-start | bytes 12292
  215.0 95.3 %copy-start.65 = (f32[1024]{0:T(1024)}, f32[1024]{0:T(1024)S(1)}, u32[]{:S(2)}) copy-start(f32[1024]{0:T(1024)S(1)} %fusion.96) | copy-start | bytes 12292
  253.7 64.7 %copy-start.15 = (bf16[256,1024]{1,0:T(8,128)(2,1)}, bf16[256,1024]{1,0:T(8,128)(2,1)S(1)}, u32[]{:S(2)}) copy-start(bf16[256,1024]{1,0:T(8,128)(2,1)S(1)} %all_gather.44) | copy-start | bytes 1572868
  296.6 13.6 %copy-start.36 = (bf16[1024,256]{0,1:T(8,128)(2,1)}, bf16[1024,256]{0,1:T(8,128)(2,1)S(1)}, u32[]{:S(2)}) copy-start(bf16[1024,256]{0,1:T(8,128)(2,1)S(1)} %convolution_convert_fusion.5) | copy-start | bytes 1572868
  310.3 7.6 %copy-start.83 = (f32[4,1024]{1,0:T(4,128)}, f32[4,1024]{1,0:T(4,128)S(1)}, u32[]{:S(2)}) copy-start(f32[4,1024]{1,0:T(4,128)S(1)} %get-tuple-element.208) | copy-start | bytes 49156
  310.3 8.1 %copy-start.99 = (f32[256]{0:T(256)S(1)}, f32[256]{0:T(256)}, u32[]{:S(2)}) copy-start(f32[256]{0:T(256)} %convert_element_type.446) | copy-start | bytes 3076
  322.9 16.9 %copy-start.48 = (f32[1024]{0:T(1024)}, f32[1024]{0:T(1024)S(1)}, u32[]{:S(2)}) copy-start(f32[1024]{0:T(1024)S(1)} %fusion.98) | copy-start | bytes 12292
  323.1 16.6 %copy-start = (bf16[1024,256]{0,1:T(8,128)(2,1)}, bf16[1024,256]{0,1:T(8,128)(2,1)S(1)}, u32[]{:S(2)}) copy-start(bf16[1024,256]{0,1:T(8,128)(2,1)S(1)} %add_convert_fusion.2) | copy-start | bytes 1572868
  323.5 16.3 %copy-start.22 = (bf16[1024,256]{0,1:T(8,128)(2,1)}, bf16[1024,256]{0,1:T(8,128)(2,1)S(1)}, u32[]{:S(2)}) copy-start(bf16[1024,256]{0,1:T(8,128)(2,1)S(1)} %convolution_convert_fusion.2) | copy-start | bytes 1572868
  339.8 9.1 %copy-start.71 = (f32[256]{0:T(256)S(1)}, f32[256]{0:T(256)}, u32[]{:S(2)}) copy-start(f32[256]{0:T(256)} %copy-done.70) | copy-start | bytes 3076
  339.8 9.1 %copy-start.100 = (f32[256]{0:T(256)S(1)}, f32[256]{0:T(256)}, u32[]{:S(2)}) copy-start(f32[256]{0:T(256)} %convert_element_type.446) | copy-start | bytes 3076
  363.4 8.9 %copy-start.14 = (bf16[1024,256]{0,1:T(8,128)(2,1)}, bf16[1024,256]{0,1:T(8,128)(2,1)S(1)}, u32[]{:S(2)}) copy-start(bf16[1024,256]{0,1:T(8,128)(2,1)S(1)} %fusion.89) | copy-start | bytes 1572868
  363.8 8.5 %copy-start.42 = (bf16[1024,256]{0,1:T(8,128)(2,1)S(1)}, bf16[1024,256]{0,1:T(8,128)(2,1)}, u32[]{:S(2)}) copy-start(bf16[1024,256]{0,1:T(8,128)(2,1)} %convolution_convert_fusion.4) | copy-start | bytes 1572868
  372.3 27.7 %copy-start.21 = (bf16[4,64,1024]{2,1,0:T(8,128)(2,1)}, bf16[4,64,1024]{2,1,0:T(8,128)(2,1)S(1)}, u32[]{:S(2)}) copy-start(bf16[4,64,1024]{2,1,0:T(8,128)(2,1)S(1)} %fusion.58) | copy-start | bytes 1572868
  383.0 11.9 %copy-start.24 = (bf16[1024,256]{0,1:T(8,128)(2,1)S(1)}, bf16[1024,256]{0,1:T(8,128)(2,1)}, u32[]{:S(2)}) copy-start(bf16[1024,256]{0,1:T(8,128)(2,1)} %convolution_convert_fusion.3) | copy-start | bytes 1572868
  404.7 70.0 %all-to-all-start.9 = ((bf16[16,1,16]{2,1,0:T(2,128)(2,1)}), bf16[16,1,16]{2,1,0:T(2,128)(2,1)}, u32[]{:S(2)}, u32[]{:S(2)}) async-start(bf16[16,1,16]{2,1,0:T(2,128)(2,1)} %convert_element_type.538), calls=%async_computation.9 | async-start | bytes 16384 | tf_op jit(solution)/shard_map/all_to_all | solution.py:22
  415.5 6.5 %copy-start.17 = (bf16[256,1024]{1,0:T(8,128)(2,1)S(1)}, bf16[256,1024]{1,0:T(8,128)(2,1)}, u32[]{:S(2)}) copy-start(bf16[256,1024]{1,0:T(8,128)(2,1)} %copy-done.15) | copy-start | bytes 1572868
  422.0 7.2 %copy-start.59 = (f32[1024]{0:T(1024)S(1)}, f32[1024]{0:T(1024)}, u32[]{:S(2)}) copy-start(f32[1024]{0:T(1024)} %copy-done.58) | copy-start | bytes 12292
  424.3 6.5 %copy-start.6 = (bf16[1,1024,256]{1,2,0:T(8,128)(2,1)S(1)}, bf16[1,1024,256]{1,2,0:T(8,128)(2,1)}, u32[]{:S(2)}) copy-start(bf16[1,1024,256]{1,2,0:T(8,128)(2,1)} %copy.115) | copy-start | bytes 1572868
  424.3 6.5 %copy-start.82 = (pred[1024]{0:T(1024)(128)(4,1)S(1)}, pred[1024]{0:T(1024)(128)(4,1)}, u32[]{:S(2)}) copy-start(pred[1024]{0:T(1024)(128)(4,1)} %get-tuple-element.206) | copy-start | bytes 3076
  424.3 6.5 %copy-start.89 = (pred[1024]{0:T(1024)(128)(4,1)S(1)}, pred[1024]{0:T(1024)(128)(4,1)}, u32[]{:S(2)}) copy-start(pred[1024]{0:T(1024)(128)(4,1)} %get-tuple-element.207) | copy-start | bytes 3076
  430.7 9.9 %copy-start.69 = (f32[1024]{0:T(1024)}, f32[1024]{0:T(1024)S(1)}, u32[]{:S(2)}) copy-start(f32[1024]{0:T(1024)S(1)} %negate_multiply_fusion.1) | copy-start | bytes 12292
  432.1 8.5 %copy-start.108 = (bf16[1024,256]{0,1:T(8,128)(2,1)S(1)}, bf16[1024,256]{0,1:T(8,128)(2,1)}, u32[]{:S(2)}) copy-start(bf16[1024,256]{0,1:T(8,128)(2,1)} %convolution_convert_fusion.7) | copy-start | bytes 1572868
  451.1 11.9 %copy-start.38 = (bf16[1024,256]{0,1:T(8,128)(2,1)S(1)}, bf16[1024,256]{0,1:T(8,128)(2,1)}, u32[]{:S(2)}) copy-start(bf16[1024,256]{0,1:T(8,128)(2,1)} %convolution_convert_fusion.6) | copy-start | bytes 1572868
  471.0 10.5 %copy-start.90 = (f32[256]{0:T(256)S(1)}, f32[256]{0:T(256)}, u32[]{:S(2)}) copy-start(f32[256]{0:T(256)} %get-tuple-element.167) | copy-start | bytes 3076
  471.0 10.5 %copy-start.92 = (f32[256]{0:T(256)S(1)}, f32[256]{0:T(256)}, u32[]{:S(2)}) copy-start(f32[256]{0:T(256)} %get-tuple-element.165) | copy-start | bytes 3076
  471.0 21.2 %copy-start.93 = (f32[256]{0:T(256)S(1)}, f32[256]{0:T(256)}, u32[]{:S(2)}) copy-start(f32[256]{0:T(256)} %get-tuple-element.173) | copy-start | bytes 3076
  471.0 31.8 %copy-start.91 = (f32[256]{0:T(256)S(1)}, f32[256]{0:T(256)}, u32[]{:S(2)}) copy-start(f32[256]{0:T(256)} %get-tuple-element.163) | copy-start | bytes 3076
  471.0 42.5 %copy-start.97 = (f32[1024]{0:T(1024)S(1)}, f32[1024]{0:T(1024)}, u32[]{:S(2)}) copy-start(f32[1024]{0:T(1024)} %get-tuple-element.227) | copy-start | bytes 12292
  471.0 42.5 %copy-start.98 = (f32[1024]{0:T(1024)S(1)}, f32[1024]{0:T(1024)}, u32[]{:S(2)}) copy-start(f32[1024]{0:T(1024)} %get-tuple-element.229) | copy-start | bytes 12292
  471.0 53.2 %copy-start.1 = (bf16[1024,256]{0,1:T(8,128)(2,1)S(1)}, bf16[1024,256]{0,1:T(8,128)(2,1)}, u32[]{:S(2)}) copy-start(bf16[1024,256]{0,1:T(8,128)(2,1)} %copy-done) | copy-start | bytes 1572868
  471.1 64.5 %copy-start.54 = (f32[256]{0:T(256)S(1)}, f32[256]{0:T(256)}, u32[]{:S(2)}) copy-start(f32[256]{0:T(256)} %copy-done.50) | copy-start | bytes 3076
  471.1 64.5 %copy-start.67 = (f32[1024]{0:T(1024)S(1)}, f32[1024]{0:T(1024)}, u32[]{:S(2)}) copy-start(f32[1024]{0:T(1024)} %copy-done.65) | copy-start | bytes 12292
  471.1 64.5 %copy-start.105 = (f32[256]{0:T(256)S(1)}, f32[256]{0:T(256)}, u32[]{:S(2)}) copy-start(f32[256]{0:T(256)} %copy-done.102) | copy-start | bytes 3076
  472.0 63.6 %copy-start.63 = (f32[1024]{0:T(1024)}, f32[1024]{0:T(1024)S(1)}, u32[]{:S(2)}) copy-start(f32[1024]{0:T(1024)S(1)} %multiply_multiply_fusion.4) | copy-start | bytes 12292
  474.7 14.0 %all-to-all-start.7 = ((bf16[16,1,16]{2,1,0:T(2,128)(2,1)}), bf16[16,1,16]{2,1,0:T(2,128)(2,1)S(1)}, u32[]{:S(2)}, u32[]{:S(2)}) async-start(bf16[16,1,16]{2,1,0:T(2,128)(2,1)} %convert_element_type.536), calls=%async_computation.7 | async-start | bytes 16384 | tf_op jit(solution)/shard_map/all_to_all | solution.py:22
  488.7 46.9 %copy-start.75 = (bf16[16,1,16]{2,1,0:T(2,128)(2,1)}, bf16[16,1,16]{2,1,0:T(2,128)(2,1)S(1)}, u32[]{:S(2)}) copy-start(bf16[16,1,16]{2,1,0:T(2,128)(2,1)S(1)} %all-to-all-done.7) | copy-start | bytes 1540
  488.7 10.6 %all-to-all-start.6 = ((bf16[16,1,16]{2,1,0:T(2,128)(2,1)}), bf16[16,1,16]{2,1,0:T(2,128)(2,1)S(1)}, u32[]{:S(2)}, u32[]{:S(2)}) async-start(bf16[16,1,16]{2,1,0:T(2,128)(2,1)} %convert_element_type.535), calls=%async_computation.6 | async-start | bytes 16384 | tf_op jit(solution)/shard_map/all_to_all | solution.py:22
  499.3 36.2 %copy-start.76 = (bf16[16,1,16]{2,1,0:T(2,128)(2,1)}, bf16[16,1,16]{2,1,0:T(2,128)(2,1)S(1)}, u32[]{:S(2)}) copy-start(bf16[16,1,16]{2,1,0:T(2,128)(2,1)S(1)} %all-to-all-done.6) | copy-start | bytes 1540
  499.3 10.7 %all-to-all-start.5 = ((bf16[16,1,16]{2,1,0:T(2,128)(2,1)}), bf16[16,1,16]{2,1,0:T(2,128)(2,1)S(1)}, u32[]{:S(2)}, u32[]{:S(2)}) async-start(bf16[16,1,16]{2,1,0:T(2,128)(2,1)} %convert_element_type.534), calls=%async_computation.5 | async-start | bytes 16384 | tf_op jit(solution)/shard_map/all_to_all | solution.py:22
  510.1 25.5 %copy-start.77 = (bf16[16,1,16]{2,1,0:T(2,128)(2,1)}, bf16[16,1,16]{2,1,0:T(2,128)(2,1)S(1)}, u32[]{:S(2)}) copy-start(bf16[16,1,16]{2,1,0:T(2,128)(2,1)S(1)} %all-to-all-done.5) | copy-start | bytes 1540
  510.1 10.6 %all-to-all-start.4 = ((bf16[16,1,16]{2,1,0:T(2,128)(2,1)}), bf16[16,1,16]{2,1,0:T(2,128)(2,1)S(1)}, u32[]{:S(2)}, u32[]{:S(2)}) async-start(bf16[16,1,16]{2,1,0:T(2,128)(2,1)} %convert_element_type.533), calls=%async_computation.4 | async-start | bytes 16384 | tf_op jit(solution)/shard_map/all_to_all | solution.py:22
  520.7 14.9 %copy-start.78 = (bf16[16,1,16]{2,1,0:T(2,128)(2,1)}, bf16[16,1,16]{2,1,0:T(2,128)(2,1)S(1)}, u32[]{:S(2)}) copy-start(bf16[16,1,16]{2,1,0:T(2,128)(2,1)S(1)} %all-to-all-done.4) | copy-start | bytes 1540
  520.7 10.6 %all-to-all-start.8 = ((bf16[16,1,64]{2,1,0:T(2,128)(2,1)}), bf16[16,1,64]{2,1,0:T(2,128)(2,1)S(1)}, u32[]{:S(2)}, u32[]{:S(2)}) async-start(bf16[16,1,64]{2,1,0:T(2,128)(2,1)} %convert_element_type.537), calls=%async_computation.8 | async-start | bytes 16384 | tf_op jit(solution)/shard_map/all_to_all | solution.py:22
  525.6 21.3 %copy-start.7 = (bf16[1,1024,256]{1,2,0:T(8,128)(2,1)S(1)}, bf16[1,1024,256]{1,2,0:T(8,128)(2,1)}, u32[]{:S(2)}) copy-start(bf16[1,1024,256]{1,2,0:T(8,128)(2,1)} %copy.115) | copy-start | bytes 1572868
  531.4 12.0 %all-to-all-start.1 = ((bf16[16,256,16]{1,2,0:T(8,128)(2,1)}), bf16[16,256,16]{1,2,0:T(8,128)(2,1)}, u32[]{:S(2)}, u32[]{:S(2)}) async-start(bf16[16,256,16]{1,2,0:T(8,128)(2,1)} %bitcast.44), calls=%async_computation.1 | async-start | bytes 262144 | tf_op jit(solution)/shard_map/all_to_all | solution.py:22
  543.4 13.2 %all-to-all-start = ((bf16[16,16,768]{2,1,0:T(8,128)(2,1)}), bf16[16,16,768]{2,1,0:T(8,128)(2,1)S(1)}, u32[]{:S(2)}, u32[]{:S(2)}) async-start(bf16[16,16,768]{2,1,0:T(8,128)(2,1)} %bitcast.215), calls=%async_computation | async-start | bytes 786432 | tf_op jit(solution)/shard_map/all_to_all | solution.py:22
  556.5 15.3 %all-to-all-start.3 = ((bf16[16,1024,16]{1,2,0:T(8,128)(2,1)}), bf16[16,1024,16]{1,2,0:T(8,128)(2,1)}, u32[]{:S(2)}, u32[]{:S(2)}) async-start(bf16[16,1024,16]{1,2,0:T(8,128)(2,1)} %bitcast.223), calls=%async_computation.3 | async-start | bytes 1048576 | tf_op jit(solution)/shard_map/all_to_all | solution.py:22
  563.6 12.5 %copy-start.86 = (f32[1024]{0:T(1024)S(1)}, f32[1024]{0:T(1024)}, u32[]{:S(2)}) copy-start(f32[1024]{0:T(1024)} %get-tuple-element.170) | copy-start | bytes 12292
  571.8 21.6 %all-to-all-start.2 = ((bf16[16,16,1024]{2,1,0:T(8,128)(2,1)}), bf16[16,16,1024]{2,1,0:T(8,128)(2,1)}, u32[]{:S(2)}, u32[]{:S(2)}) async-start(bf16[16,16,1024]{2,1,0:T(8,128)(2,1)} %bitcast.220), calls=%async_computation.2 | async-start | bytes 1048576 | tf_op jit(solution)/shard_map/all_to_all | solution.py:22
  576.0 40.1 %all-reduce.10.cloned.1.call-start = ((), (), s32[]{:S(2)}) async-start(), calls=%async_computation.10 | async-start | bytes 202752 | tf_op jit(solution)/shard_map/psum | solution.py:341
  576.7 18.5 %copy-start.9 = (f32[1024,256]{0,1:T(8,128)S(1)}, f32[1024,256]{0,1:T(8,128)}, u32[]{:S(2)}) copy-start(f32[1024,256]{0,1:T(8,128)} %copy-done.8) | copy-start | bytes 3145732
  576.7 18.5 %copy-start.55 = (f32[256]{0:T(256)S(1)}, f32[256]{0:T(256)}, u32[]{:S(2)}) copy-start(f32[256]{0:T(256)} %copy-done.50) | copy-start | bytes 3076
  576.7 18.5 %copy-start.64 = (f32[1024]{0:T(1024)S(1)}, f32[1024]{0:T(1024)}, u32[]{:S(2)}) copy-start(f32[1024]{0:T(1024)} %copy-done.63) | copy-start | bytes 12292
  576.7 18.5 %copy-start.68 = (f32[1024]{0:T(1024)S(1)}, f32[1024]{0:T(1024)}, u32[]{:S(2)}) copy-start(f32[1024]{0:T(1024)} %copy-done.65) | copy-start | bytes 12292
  581.9 15.6 %copy-start.41 = (bf16[1,1024,256]{1,2,0:T(8,128)(2,1)S(1)}, bf16[1,1024,256]{1,2,0:T(8,128)(2,1)}, u32[]{:S(2)}) copy-start(bf16[1,1024,256]{1,2,0:T(8,128)(2,1)} %fusion.70) | copy-start | bytes 1572868
  (60 other events, 159.8 us)
Sparse Core Ops, SparseCore 0:
  595.3 20.8 all-reduce.9
where the time goes:
time: 644 us; the launch traced here: 638 us
  blocking collectives  275 us (43%)
  matrix products  143 us (22%)
  other arithmetic  72.5 us (11%)
  waiting for transfers between devices  62 us (10%)
  starting transfers between devices  41.3 us (6%)
  local copies, waits for them, and re-layouts  27.1 us (4%)
  between operations  17.6 us (3%)
    all_to_all x10, waiting for transfers between devices, summed_on_arrival(): lax.all_to_all(split_up(shard, dim, devices), axis, 0, 0, tiled=True)  45.4 us
    unnamed x1, blocking collectives  44 us
    all_gather x1, blocking collectives, on_device(): lax.all_gather(w_down, 'wide', axis=1, tiled=True)  42.4 us
    all_to_all x10, starting transfers between devices, summed_on_arrival(): lax.all_to_all(split_up(shard, dim, devices), axis, 0, 0, tiled=True)  41.3 us
    all_gather x1, blocking collectives, on_device(): lax.all_gather(w_up, 'wide', axis=0, tiled=True)  38.7 us
    all_gather x1, blocking collectives, on_device(): lax.all_gather(w_out, 'wide', axis=1, tiled=True)  38.5 us
    all_gather x1, blocking collectives, on_device(): lax.all_gather(w_key, 'wide', axis=0, tiled=True)  38.3 us
    all_gather x1, blocking collectives, on_device(): lax.all_gather(w_value, 'wide', axis=0, tiled=True)  36.4 us
  transfers between devices with their start and end apart: 11, of which 9 were waited for; matrix products, arithmetic and copies ran while one was open for 16% of the time, Pallas kernels for 0%

commit v1 on v0

v1 whole, which is shorter than its diff:
```python
import functools
import math

import jax
import jax.numpy as jnp
from jax import lax
from jax.experimental import pallas as pl
from jax.experimental.pallas import tpu as pltpu
from jax.sharding import PartitionSpec as P

F32, BF = jnp.float32, jnp.bfloat16
MESH = pl.DeviceIdType.MESH
HEADS = 4
NORM_EPS = 1e-05
MASK_FILL = -1e30
C = 256
QB = 128
NN = (((1,), (0,)), ((), ()))
NT = (((1,), (1,)), ((), ()))
TN = (((0,), (0,)), ((), ()))
C0 = math.sqrt(2 / math.pi)
C1 = C0 * 0.044715

SMALL, WQ, WK, WV, WO, WU, WD = 0, 1, 2, 3, 4, 5, 10
SLABS = 14
GROUP_A, GROUP_B, GROUP_C = (0, 2), (4, 3), (10, 2)


def dot(a, b, dims=NN):
    return lax.dot_general(a, b, dims, preferred_element_type=F32)


class Exchange:
    def __init__(self, line, plane):
        self.line, self.plane = line, plane
        self.n = line * plane
        self.core = lax.axis_index("dp")
        self.me = lax.axis_index("wide")
        self.a = self.me // plane
        self.p = self.me % plane

    def chip(self, a, p):
        return {"dp": self.core, "wide": a * self.plane + p}

    def sibling(self):
        return {"dp": 1 - self.core, "wide": self.me}

    def along(self, step):
        return lax.rem(self.a + step, self.line)

    def across(self, step):
        return lax.rem(self.p + step, self.plane)


def send(src, dst, sems, k, device):
    copy = pltpu.make_async_remote_copy(
        src_ref=src,
        dst_ref=dst,
        send_sem=sems[0].at[k],
        recv_sem=sems[1].at[k],
        device_id=device,
        device_id_type=MESH,
    )
    copy.start()
    return copy


def arrived(copies):
    for copy in copies:
        copy.wait_recv()


def left(copies):
    for copy in copies:
        copy.wait_send()


def body(names, line, plane, r, *refs):
    s = dict(zip(names, refs))
    tok, cot, lens, cnts = s["tok"], s["cot"], s["lens"], s["cnts"]
    out, ing, res = s["out"], s["ing"], s["res"]
    wb, G, gs, small = s["wb"], s["G"], s["gs"], s["small"]
    gb = s.get("gb", wb)
    S, D = tok.shape
    nb = S // QB
    n = line * plane
    rp = wb.shape[3]
    x = Exchange(line, plane)
    core, me = x.core, x.me

    barrier = pltpu.get_barrier_semaphore()
    pl.semaphore_signal(barrier, inc=1, device_id=x.sibling(), device_id_type=MESH)
    for k in range(1, n):
        pl.semaphore_signal(
            barrier,
            inc=1,
            device_id={"dp": core, "wide": lax.rem(me + k, n)},
            device_id_type=MESH,
        )

    lanes = lax.broadcasted_iota(jnp.int32, (16, D), 1)
    rows16 = lax.broadcasted_iota(jnp.int32, (16, D), 0)
    tile = s["tile"]
    tile[...] = jnp.zeros((16, D), F32)
    for i, key in enumerate(("g1", "s1", "g2", "s2", "bd")):
        tile[i : i + 1, 0:r] = s[key][...].astype(F32)
    own = pltpu.roll(tile[...], me * r, axis=1)
    tile[0:1, 0 : 4 * r] = s["bu"][...].astype(F32)
    ups = jnp.broadcast_to(tile[0:1, :], (16, D))
    ups = jnp.where((lanes < 4 * r) & (rows16 == 5 + (me * 4 * r) // D), ups, 0.0)
    small_own = jnp.where(rows16 < 5, own, pltpu.roll(ups, lax.rem(me * 4 * r, D), axis=1)).astype(BF)
    first = jnp.where(core == 0, 1.0, 0.0).astype(BF)
    second = jnp.where(core == 0, 0.0, 1.0).astype(BF)

    def pad(v):
        return v if rp == r else jnp.concatenate([v.astype(F32), jnp.zeros((rp - r, D), F32)], axis=0).astype(BF)

    up = [pad(s["up"][:, c * D : (c + 1) * D]) for c in range(4)]
    down = [pad(s["down"][:, c * D : (c + 1) * D]) for c in range(4)]
    q_own, k_own, v_own, o_own = (pad(s[key][...]) for key in ("wq", "wk", "wv", "wo"))
    for (base, half), parts in (
        (GROUP_A, ((small_own, k_own), (q_own, v_own))),
        (GROUP_B, ((o_own, up[2]), (up[0], up[3]), (up[1], up[3]))),
        (GROUP_C, ((down[0], down[2]), (down[1], down[3]))),
    ):
        for i, (of_first, of_second) in enumerate(parts):
            wb[base + half * core + i, x.a, x.p] = of_first * first + of_second * second

    slot = lax.broadcasted_iota(jnp.int32, (nb, QB), 0) * QB + lax.broadcasted_iota(jnp.int32, (nb, QB), 1)
    end = jnp.int32(0)
    start_of = jnp.zeros((nb, QB), jnp.int32)
    loops_of = jnp.zeros((nb, QB), jnp.int32)
    for j in range(lens.shape[1]):
        inside = slot >= end
        start_of = jnp.where(inside, end, start_of)
        loops_of = jnp.where(inside, cnts[0, j], loops_of)
        end = end + lens[0, j]
    start_t = jnp.transpose(start_of.astype(F32))
    loops_t = jnp.transpose(loops_of.astype(F32))
    kk = lax.broadcasted_iota(jnp.int32, (QB, 2 * QB), 1).astype(F32)
    qq = lax.broadcasted_iota(jnp.int32, (QB, 2 * QB), 0).astype(F32)
    for b in range(nb):
        ok = (kk >= start_t[:, b : b + 1] - (b - 1) * QB) & (kk <= qq + QB)
        if b == 0:
            ok = ok & (kk >= QB)
        s["mask"][b] = jnp.where(ok, 0.0, MASK_FILL)
        s["act"][pl.ds(b * QB, QB), :] = jnp.broadcast_to(
            jnp.where(loops_t[:, b : b + 1] > 1, 1.0, 0.0), (QB, 128)
        )
    lane_head = lax.broadcasted_iota(jnp.int32, (1, D), 1) // (D // HEADS)
    hm = [jnp.where(lane_head == h, 1.0, 0.0).astype(BF) for h in range(HEADS)]
    for t in range(2):
        s["k"][t, 0:QB, :] = jnp.zeros((QB, D), BF)
        s["v"][t, 0:QB, :] = jnp.zeros((QB, D), BF)
    G[...] = jnp.zeros(G.shape, F32)
    gs[...] = jnp.zeros(gs.shape, F32)

    pl.semaphore_wait(barrier, n)

    def mine(group, buf=wb):
        base, half = group
        return buf.at[pl.ds(base + half * core, half)]

    sem = {key: (s["send_" + key], s["recv_" + key]) for key in SEMS(line, plane)}
    to_a = [
        send(mine(GROUP_A).at[:, x.a, x.p], mine(GROUP_A).at[:, x.a, x.p], sem["a"], k - 1,
             {"dp": core, "wide": lax.rem(me + k, n)})
        for k in range(1, n)
    ]
    to_b = [
        send(mine(GROUP_B).at[:, x.a, x.p], mine(GROUP_B).at[:, x.a, x.p], sem["b1"], k - 1,
             x.chip(x.along(k), x.p))
        for k in range(1, line)
    ]
    to_c = [
        send(mine(GROUP_C).at[:, x.a, x.p], mine(GROUP_C).at[:, x.a, x.p], sem["c1"], k - 1,
             x.chip(x.a, x.across(k)))
        for k in range(1, plane)
    ]
    arrived(to_a)
    share_a = [send(mine(GROUP_A), mine(GROUP_A), sem["sib"], 0, x.sibling())]
    arrived(to_b)
    to_b2 = [
        send(mine(GROUP_B).at[:, :, x.p], mine(GROUP_B).at[:, :, x.p], sem["b2"], k - 1,
             x.chip(x.a, x.across(k)))
        for k in range(1, plane)
    ]
    arrived(to_c)
    to_c2 = [
        send(mine(GROUP_C).at[:, x.a], mine(GROUP_C).at[:, x.a], sem["c2"], k - 1,
             x.chip(x.along(k), x.p))
        for k in range(1, line)
    ]
    arrived(share_a)
    whole_small = wb[SMALL].reshape(n, rp, D).astype(F32)
    small[...] = jnp.sum(whole_small, axis=0)[0:16]

    def W(i):
        return wb[i].reshape(D, D) if rp == r else s["wf"][i]

    def places():
        row = lax.broadcasted_iota(jnp.int32, (D, n * rp), 0)
        place = lax.broadcasted_iota(jnp.int32, (D, n * rp), 1)
        return jnp.where(place == (row // r) * rp + lax.rem(row, r), 1.0, 0.0).astype(BF)

    def unpack(base, count):
        if rp != r:

            @pl.loop(base, base + count)
            def _(i):
                s["wf"][i] = dot(places(), wb[i].reshape(n * rp, D)).astype(BF)

    def wide(v):
        return jnp.concatenate([v, v], axis=1)

    def norm_fwd(v, g, b):
        mean = jnp.mean(v, axis=1, keepdims=True)
        cen = v - mean
        var = jnp.mean(cen * cen, axis=1, keepdims=True)
        rstd = lax.rsqrt(var + NORM_EPS)
        z = cen * rstd
        return z, rstd, (z * g + b).astype(BF)

    def forward_attention(t, i):
        r0 = pl.multiple_of(i * C, C)
        rows = pl.ds(r0, C)
        tk = tok[rows, :].astype(F32)
        mixed = tk + tk if t == 0 else s["state"][rows, :] + tk
        z1, r1, n1 = norm_fwd(mixed, small[0:1, :], small[1:2, :])
        s["z1"][t, rows, :] = z1
        s["r1"][t, rows, :] = jnp.broadcast_to(r1, (C, 128))
        s["n1"][t, rows, :] = n1
        q = dot(n1, W(WQ)).astype(BF)
        s["q"][t, rows, :] = q
        s["k"][t, pl.ds(r0 + QB, C), :] = dot(n1, W(WK)).astype(BF)
        s["v"][t, pl.ds(r0 + QB, C), :] = dot(n1, W(WV)).astype(BF)
        for u in range(C // QB):
            b = i * (C // QB) + u
            win = pl.ds(pl.multiple_of(b * QB, QB), 2 * QB)
            kw, vw = s["k"][t, win, :], s["v"][t, win, :]
            qb = q[u * QB : (u + 1) * QB]
            qs = jnp.concatenate([qb * hm[h] for h in range(HEADS)], axis=0)
            sc = dot(qs, kw, NT)
            mask = s["mask"][b]
            ps = []
            for h in range(HEADS):
                e = sc[h * QB : (h + 1) * QB] * (D // HEADS) ** -0.5 + mask
                e = jnp.exp(e - jnp.max(e, axis=1, keepdims=True))
                ps.append((e * (1.0 / jnp.sum(e, axis=1, keepdims=True))).astype(BF))
            p = jnp.concatenate(ps, axis=0)
            s["p"][t, b] = p
            o = dot(p, vw)
            at = o[0:QB]
            for h in range(1, HEADS):
                at = jnp.where(lane_head == h, o[h * QB : (h + 1) * QB], at)
            s["at"][t, pl.ds(pl.multiple_of(b * QB, QB), QB), :] = at.astype(BF)
        s["mixed"][rows, :] = mixed

    def forward_hidden(t, i):
        rows = pl.ds(pl.multiple_of(i * C, C), C)
        resid = s["mixed"][rows, :] + dot(s["at"][t, rows, :], W(WO), NT)
        z2, r2, n2 = norm_fwd(resid, small[2:3, :], small[3:4, :])
        s["z2"][t, rows, :] = z2
        s["r2"][t, rows, :] = jnp.broadcast_to(r2, (C, 128))
        s["n2"][t, rows, :] = n2
        acc = resid + small[4:5, :]
        for c in range(4):
            hp = dot(n2, W(WU + c)) + small[5 + c : 6 + c, :]
            v2 = hp * hp
            th = jnp.tanh(hp * (C1 * v2 + C0))
            pr = 0.5 * th + 0.5
            g = hp * pr
            d = pr + g * (1.0 - pr) * ((6 * C1) * v2 + (2 * C0))
            g = g.astype(BF)
            s["h"][t, c, rows, :] = g
            s["d"][t, c, rows, :] = d.astype(BF)
            acc = acc + dot(g, W(WD + c), NT)
        if t == 0:
            s["state"][rows, :] = acc
        else:
            act = wide(s["act"][rows, :])
            out[rows, :] = jnp.where(act > 0, acc, s["state"][rows, :]).astype(BF)

    def norm_bwd(dn, g, z, rstd, gi):
        e = dn * g
        gs[gi : gi + 1, :] += jnp.sum(dn * z, axis=0, keepdims=True)
        gs[gi + 1 : gi + 2, :] += jnp.sum(dn, axis=0, keepdims=True)
        m1 = jnp.mean(e, axis=1, keepdims=True)
        m2 = jnp.mean(e * z, axis=1, keepdims=True)
        return wide(rstd) * (e - m1 - z * m2)

    def backward_hidden(t, i):
        rows = pl.ds(pl.multiple_of(i * C, C), C)
        if t == 1:
            br = jnp.where(wide(s["act"][rows, :]) > 0, cot[rows, :].astype(F32), 0.0)
        else:
            br = s["state"][rows, :]
        b2 = br.astype(BF)
        gs[4:5, :] += jnp.sum(br, axis=0, keepdims=True)
        b2t = b2.T
        n2t = s["n2"][t, rows, :].T
        dn2 = jnp.zeros((C, D), F32)
        for c in range(4):
            G[WD + c] += dot(b2t, s["h"][t, c, rows, :])
            dp = s["d"][t, c, rows, :].astype(F32) * dot(b2, W(WD + c))
            gs[5 + c : 6 + c, :] += jnp.sum(dp, axis=0, keepdims=True)
            dp = dp.astype(BF)
            G[WU + c] += dot(n2t, dp)
            dn2 = dn2 + dot(dp, W(WU + c), NT)
        bres = br + norm_bwd(dn2, small[2:3, :], s["z2"][t, rows, :], s["r2"][t, rows, :], 2)
        s["bres"][rows, :] = bres
        b1 = bres.astype(BF)
        G[WO] += dot(b1.T, s["at"][t, rows, :])
        s["do"][rows, :] = dot(b1, W(WO)).astype(BF)

    def backward_attention(t, i):
        r0 = pl.multiple_of(i * C, C)
        rows = pl.ds(r0, C)
        for u in reversed(range(C // QB)):
            b = i * (C // QB) + u
            win = pl.ds(pl.multiple_of(b * QB, QB), 2 * QB)
            qrows = pl.ds(pl.multiple_of(b * QB, QB), QB)
            kw, vw = s["k"][t, win, :], s["v"][t, win, :]
            qb, dob = s["q"][t, qrows, :], s["do"][qrows, :]
            qs = jnp.concatenate([qb * hm[h] for h in range(HEADS)], axis=0)
            dos = jnp.concatenate([dob * hm[h] for h in range(HEADS)], axis=0)
            p = s["p"][t, b]
            dp = dot(dos, vw, NT)
            pf = p.astype(F32)
            tt = pf * dp
            ds_ = (tt - pf * jnp.sum(tt, axis=1, keepdims=True)).astype(BF)
            dq = dot(ds_, kw)
            a = dq[0:QB]
            for h in range(1, HEADS):
                a = jnp.where(lane_head == h, dq[h * QB : (h + 1) * QB], a)
            s["dq"][pl.ds(u * QB, QB), :] = (a * (D // HEADS) ** -0.5).astype(BF)
            s["dv"][win, :] += dot(p, dos, TN)
            s["dk"][win, :] += dot(ds_, qs, TN)
        dq = s["dq"][...]
        own_keys = pl.ds(r0 + QB, C)
        dk = (s["dk"][own_keys, :] * (D // HEADS) ** -0.5).astype(BF)
        dv = s["dv"][own_keys, :].astype(BF)
        n1t = s["n1"][t, rows, :].T
        G[WQ] += dot(n1t, dq)
        G[WK] += dot(n1t, dk)
        G[WV] += dot(n1t, dv)
        dn1 = dot(dq, W(WQ), NT) + dot(dk, W(WK), NT) + dot(dv, W(WV), NT)
        bm = s["bres"][rows, :] + norm_bwd(dn1, small[0:1, :], s["z1"][t, rows, :], s["r1"][t, rows, :], 0)
        if t == 1:
            s["bi"][rows, :] = bm
            s["state"][rows, :] = jnp.where(wide(s["act"][rows, :]) > 0, 0.0, cot[rows, :].astype(F32)) + bm
        else:
            ing[rows, :] = (s["bi"][rows, :] + 2.0 * bm).astype(BF)

    chunks = S // C
    unpack(WQ, 3)

    @pl.loop(0, chunks)
    def _(i):
        forward_attention(0, i)

    arrived(to_b2)
    share_b = [send(mine(GROUP_B), mine(GROUP_B), sem["sib"], 1, x.sibling())]
    arrived(to_c2)
    share_c = [send(mine(GROUP_C), mine(GROUP_C), sem["sib"], 2, x.sibling())]
    arrived(share_b + share_c)
    unpack(WO, 5)
    unpack(WD, 4)

    @pl.loop(0, chunks)
    def _(i):
        forward_hidden(0, i)

    @pl.loop(0, chunks)
    def _(i):
        forward_attention(1, i)
        forward_hidden(1, i)

    s["dk"][...] = jnp.zeros(s["dk"].shape, F32)
    s["dv"][...] = jnp.zeros(s["dv"].shape, F32)

    @pl.loop(0, chunks)
    def _(i):
        backward_hidden(1, chunks - 1 - i)
        backward_attention(1, chunks - 1 - i)

    @pl.loop(0, chunks)
    def _(i):
        backward_hidden(0, chunks - 1 - i)

    def stage(base, count):
        @pl.loop(base, base + count)
        def _(i):
            if rp == r:
                gb[i] = G[i].astype(BF).reshape(line, plane, r, D)
            else:
                gb[i] = dot(places(), G[i].astype(BF), TN).astype(BF).reshape(line, plane, rp, D)

    def swap(group, inbox, k):
        base, half = group
        return [send(gb.at[pl.ds(base + half * (1 - core), half)], inbox, sem["rsib"], k, x.sibling())]

    def add_swapped(copies, group, inbox):
        arrived(copies)
        base, half = group
        @pl.loop(0, half)
        def _(i):
            at = base + half * core + i
            gb[at] = (gb[at].astype(F32) + inbox[i].astype(F32)).astype(BF)

    def finished(group, k, total):
        base, half = group
        for i in range(half):
            res[base + half * core + i] = total[i]
        part = res.at[pl.ds(base + half * core, half)]
        return [send(part, part, sem["fsib"], k, x.sibling())]

    left(to_a + to_b + to_c + to_b2 + to_c2 + share_a + share_b + share_c)
    stage(WO, 5)
    gb[WO + 5] = jnp.zeros(gb.shape[1:], BF)
    stage(WD, 4)
    swap_b = swap(GROUP_B, s["inb"], 1)
    swap_c = swap(GROUP_C, s["inc"], 2)

    s["dk"][...] = jnp.zeros(s["dk"].shape, F32)
    s["dv"][...] = jnp.zeros(s["dv"].shape, F32)
    backward_attention(0, chunks - 1)
    add_swapped(swap_b, GROUP_B, s["inb"])
    from_b = [
        send(mine(GROUP_B, gb).at[:, :, x.across(k)], s["inb1"].at[k - 1], sem["rb1"], k - 1,
             x.chip(x.a, x.across(k)))
        for k in range(1, plane)
    ]
    add_swapped(swap_c, GROUP_C, s["inc"])
    from_c = [
        send(mine(GROUP_C, gb).at[:, x.along(k)], s["inc1"].at[k - 1], sem["rc1"], k - 1,
             x.chip(x.along(k), x.p))
        for k in range(1, line)
    ]
    for i in range(chunks - 2, 0, -1):
        backward_attention(0, i)
    arrived(from_b)
    sum_b = mine(GROUP_B, gb)[:, :, x.p].astype(F32)
    for k in range(1, plane):
        sum_b = sum_b + s["inb1"][k - 1].astype(F32)
    s["sumb"][...] = sum_b.astype(BF)
    from_b2 = [
        send(s["sumb"].at[:, x.along(k)], s["inb2"].at[k - 1], sem["rb2"], k - 1, x.chip(x.along(k), x.p))
        for k in range(1, line)
    ]
    arrived(from_c)
    sum_c = mine(GROUP_C, gb)[:, x.a].astype(F32)
    for k in range(1, line):
        sum_c = sum_c + s["inc1"][k - 1].astype(F32)
    s["sumc"][...] = sum_c.astype(BF)
    from_c2 = [
        send(s["sumc"].at[:, x.across(k)], s["inc2"].at[k - 1], sem["rc2"], k - 1, x.chip(x.a, x.across(k)))
        for k in range(1, plane)
    ]
    backward_attention(0, 0)
    stage(WQ, 3)
    gb[SMALL] = jnp.broadcast_to(gs[...].astype(BF)[None, None], (line, plane, 16, D))
    swap_a = swap(GROUP_A, s["ina"], 0)
    arrived(from_b2)
    total = s["sumb"][:, x.a].astype(F32)
    for k in range(1, line):
        total = total + s["inb2"][k - 1].astype(F32)
    done_b = finished(GROUP_B, 1, total)
    arrived(from_c2)
    total = s["sumc"][:, x.p].astype(F32)
    for k in range(1, plane):
        total = total + s["inc2"][k - 1].astype(F32)
    done_c = finished(GROUP_C, 2, total)
    add_swapped(swap_a, GROUP_A, s["ina"])
    from_a = []
    for k in range(1, n):
        to = lax.rem(me + k, n)
        from_a.append(
            send(mine(GROUP_A, gb).at[:, to // plane, lax.rem(to, plane)], s["ina1"].at[k - 1], sem["ra"], k - 1,
                 {"dp": core, "wide": to})
        )
    arrived(from_a)
    total = mine(GROUP_A, gb)[:, x.a, x.p].astype(F32)
    for k in range(1, n):
        total = total + s["ina1"][k - 1].astype(F32)
    done_a = finished(GROUP_A, 0, total)
    arrived(done_a + done_b + done_c)
    left(swap_a + swap_b + swap_c + from_a + from_b + from_b2 + from_c + from_c2)
    left(done_a + done_b + done_c)


def SEMS(line, plane):
    n = line * plane
    return {
        "a": n - 1, "b1": line - 1, "c1": plane - 1, "b2": plane - 1, "c2": line - 1, "sib": 3,
        "rsib": 3, "rb1": plane - 1, "rb2": line - 1, "rc1": line - 1, "rc2": plane - 1, "ra": n - 1, "fsib": 3,
    }


def scratch(S, D, line, plane, rp):
    nb, n = S // QB, line * plane
    V = pltpu.VMEM
    shapes = dict(
        tile=V((16, D), F32), small=V((16, D), F32),
        wb=V((SLABS, line, plane, rp, D), BF),
        G=V((SLABS, D, D), F32), gs=V((16, D), F32),
        ina=V((2, line, plane, rp, D), BF), inb=V((3, line, plane, rp, D), BF), inc=V((2, line, plane, rp, D), BF),
        ina1=V((n - 1, 2, rp, D), BF),
        inb1=V((plane - 1, 3, line, rp, D), BF), inb2=V((line - 1, 3, rp, D), BF), sumb=V((3, line, rp, D), BF),
        inc1=V((line - 1, 2, plane, rp, D), BF), inc2=V((plane - 1, 2, rp, D), BF), sumc=V((2, plane, rp, D), BF),
        mask=V((nb, QB, 2 * QB), F32), act=V((S, 128), F32), state=V((S, D), F32), mixed=V((S, D), F32),
        z1=V((2, S, D), F32), r1=V((2, S, 128), F32), n1=V((2, S, D), BF),
        z2=V((2, S, D), F32), r2=V((2, S, 128), F32), n2=V((2, S, D), BF),
        q=V((2, S, D), BF), k=V((2, S + QB, D), BF), v=V((2, S + QB, D), BF),
        p=V((2, nb, HEADS * QB, 2 * QB), BF), at=V((2, S, D), BF),
        h=V((2, 4, S, D), BF), d=V((2, 4, S, D), BF),
        bres=V((S, D), F32), do=V((S, D), BF),
        dq=V((C, D), BF), dk=V((S + QB, D), F32), dv=V((S + QB, D), F32), bi=V((S, D), F32),
    )
    if D // n != rp:
        shapes["wf"] = V((SLABS, D, D), BF)
    else:
        shapes["gb"] = V((SLABS, line, plane, rp, D), BF)
    for key, count in SEMS(line, plane).items():
        shapes["send_" + key] = pltpu.SemaphoreType.DMA((count,))
        shapes["recv_" + key] = pltpu.SemaphoreType.DMA((count,))
    return shapes


def finish(r, *refs):
    out_in, ing_in, res, out, ing, gq, gk, gv, go, gu, gd, gg1, gs1, gg2, gs2, gbu, gbd, sems = refs
    copies = [pltpu.make_async_copy(out_in, out, sems.at[0]), pltpu.make_async_copy(ing_in, ing, sems.at[1])]
    for copy in copies:
        copy.start()
    D = res.shape[2]
    me = lax.axis_index("wide")
    for ref, at in ((gq, WQ), (gk, WK), (gv, WV), (go, WO)):
        ref[...] = res[at, 0:r, :]
    for c in range(4):
        gu[:, c * D : (c + 1) * D] = res[WU + c, 0:r, :]
        gd[:, c * D : (c + 1) * D] = res[WD + c, 0:r, :]
    tile = res[SMALL, 0:16, :]
    own = pltpu.roll(tile, lax.rem(D - me * r, D), axis=1)
    for i, ref in enumerate((gg1, gs1, gg2, gs2, gbd)):
        ref[...] = own[i : i + 1, 0:r]
    row = jnp.zeros((1, D), F32)
    for c in range(4):
        row = jnp.where((me * 4 * r) // D == c, tile[5 + c : 6 + c, :], row)
    row = jnp.broadcast_to(row, (8, D))
    gbu[...] = pltpu.roll(row, lax.rem(D - lax.rem(me * 4 * r, D), D), axis=1)[0:1, 0 : 4 * r]
    for copy in copies:
        copy.wait()


def on_device(sizes, *args):
    (tokens, lengths, counts, wq, wk, wv, wo, wu, wd, g1, s1, g2, s2, bu, bd, cot) = args
    line, plane = sizes
    S, D = tokens.shape[1:]
    r = wq.shape[0]
    rp = max(r, 16)
    vm = pl.BlockSpec(memory_space=pltpu.VMEM)
    sm = pl.BlockSpec(memory_space=pltpu.SMEM)
    hbm = pl.BlockSpec(memory_space=pl.ANY)
    inputs = dict(
        tok=tokens[0], cot=cot[0], lens=lengths, cnts=counts, wq=wq, wk=wk, wv=wv, wo=wo.T, up=wu, down=wd.T,
        g1=g1[None], s1=s1[None], g2=g2[None], s2=s2[None], bu=bu[None], bd=bd[None],
    )
    shapes = scratch(S, D, line, plane, rp)
    names = [*inputs, "out", "ing", "res", *shapes]
    out, ing, res = pl.pallas_call(
        functools.partial(body, names, line, plane, r),
        out_shape=(
            jax.ShapeDtypeStruct((S, D), BF),
            jax.ShapeDtypeStruct((S, D), BF),
            jax.ShapeDtypeStruct((SLABS, rp, D), F32),
        ),
        in_specs=[sm if key in ("lens", "cnts") else vm for key in inputs],
        out_specs=(vm, vm, vm),
        scratch_shapes=list(shapes.values()),
        compiler_params=pltpu.CompilerParams(
            collective_id=0, has_side_effects=True, vmem_limit_bytes=60 * 2**20
        ),
        name="loop_block",
    )(*inputs.values())
    f = lambda *shape: jax.ShapeDtypeStruct(shape, F32)
    out, ing, gq, gk, gv, go, gu, gd, gg1, gs1, gg2, gs2, gbu, gbd = pl.pallas_call(
        functools.partial(finish, r),
        out_shape=(
            jax.ShapeDtypeStruct((S, D), BF), jax.ShapeDtypeStruct((S, D), BF),
            f(r, D), f(r, D), f(r, D), f(r, D), f(r, 4 * D), f(r, 4 * D),
            f(1, r), f(1, r), f(1, r), f(1, r), f(1, 4 * r), f(1, r),
        ),
        in_specs=[hbm, hbm, vm],
        out_specs=(hbm, hbm) + (vm,) * 12,
        scratch_shapes=[pltpu.SemaphoreType.DMA((2,))],
        name="finish",
    )(out, ing, res)
    return (out[None], ing[None], gq, gk, gv, go.T, gu, gd.T, gg1[0], gs1[0], gg2[0], gs2[0], gbu[0], gbd[0])


def solution(mesh):
    wide = mesh.shape["wide"]
    line = 4 if wide % 4 == 0 else 1
    rows = P(("dp", "wide"), None, None)
    row = P(("dp", "wide"), None)
    first, second, one = P("wide", None), P(None, "wide"), P("wide")
    weights = (first, first, first, second, first, second)
    return jax.shard_map(
        functools.partial(on_device, (line, wide // line)),
        mesh=mesh,
        in_specs=(rows, row, row, *weights, *(one,) * 6, rows),
        out_specs=(rows, rows, *weights, *(one,) * 6),
        check_vma=False,
    )
```

time: 644 us -> 118 us (0.18)
  blocking collectives: 275 us -> 0 us
  matrix products: 143 us -> 0 us
  Pallas kernels: 0 us -> 116 us
  other arithmetic: 72.5 us -> 0 us
  waiting for transfers between devices: 62 us -> 0 us
  starting transfers between devices: 41.3 us -> 0 us
  local copies, waits for them, and re-layouts: 27.1 us -> 0 us
  between operations: 17.6 us -> 0.82 us
    all_gather x6 -> x0, blocking collectives: 231 us -> none  [the longest x1 42.4 us: on_device(): lax.all_gather(w_down, 'wide', axis=1, tiled=True)]
    dot_general x46 -> x0, matrix products: 120 us -> none  [the longest x2 21.1 us: block_backward(): jnp.einsum('qhd,khd->hqk', back_attend, values_act, preferred_element_typ...]
    pallas_call x0 -> x2, Pallas kernels: none -> 116 us  [the longest x1 81.5 us: on_device(): pl.pallas_call(functools.partial(body, names, line, plane, r), out_shape=...]
    all_to_all x10 -> x0, waiting for transfers between devices: 45.4 us -> none  [summed_on_arrival(): lax.all_to_all(split_up(shard, dim, devices), axis, 0, 0, tiled=True)]
    unnamed x1 -> x0, blocking collectives: 44 us -> none
    all_to_all x10 -> x0, starting transfers between devices: 41.3 us -> none  [summed_on_arrival(): lax.all_to_all(split_up(shard, dim, devices), axis, 0, 0, tiled=True)]
    convert_element_type x29 -> x0, other arithmetic: 41 us -> none  [the longest x2 23.8 us: block_backward(): back_scores = back_scores.astype(jnp.bfloat16)]
    reduce_sum x24 -> x0, other arithmetic: 25.5 us -> none  [the longest x10 12.6 us: summed_on_arrival(): return jnp.sum(blocks.astype(jnp.float32), axis=0)]
  transfers between devices with their start and end apart: 11 -> 0, of which waited for: 9 -> 0; matrix products, arithmetic and copies ran while one was open for 16% -> 0% of each run, Pallas kernels for 0% -> 0%
where the time goes in v1:
time: 118 us; the launch traced here: 117 us
  Pallas kernels  116 us (98%)
    pallas_call x1, Pallas kernels, on_device(): pl.pallas_call(functools.partial(body, names, line, plane, r), out_shape=...  81.5 us
    pallas_call x1, Pallas kernels, on_device(): pl.pallas_call(functools.partial(finish, r), out_shape=(jax.ShapeDtypeStr...  34.5 us

profile of v1, /device:TPU:0, one launch (start us, length us, event | category | flops | bytes accessed | tf_op | source)
XLA Modules:
  0.0 116.9 jit_solution(2959148912949871719)
XLA Ops:
  0.7 81.5 %loop_block.1 = (bf16[1024,256]{1,0:T(8,128)(2,1)}, bf16[1024,256]{1,0:T(8,128)(2,1)}, f32[14,16,256]{2,1,0:T(8,128)}) custom-call(bf16[1024,256]{1,0:T(8,128)(2,1)} %bitcast.20, bf16[1024,256]{1,0:T(8,128)(2,1)} %bitcast.21, s32[1,20]{1,0:T(1,128)} %refs_2_.1, s32[1,20]{1,0:T(1,128)} %refs_3_.1, bf16[16,256]{1,0:T(8,128)(2,1)} %refs_4_.1, ...), custom_call_target="tpu_custom_call" | custom-call | tf_op jit(solution)/shard_map/loop_block/pallas_call | solution.py:570
  82.2 34.5 %finish.1 = (bf16[1024,256]{1,0:T(8,128)(2,1)}, bf16[1024,256]{1,0:T(8,128)(2,1)}, f32[16,256]{1,0:T(8,128)}, f32[16,256]{1,0:T(8,128)}, f32[16,256]{1,0:T(8,128...) custom-call(bf16[1024,256]{1,0:T(8,128)(2,1)} %get-tuple-element.31., ...), custom_call_target="tpu_custom_call" | custom-call | tf_op jit(solution)/shard_map/finish/pallas_call | solution.py:586

commit v2 on v1

--- a/solution.py
+++ b/solution.py
@@ -528,10 +528,9 @@
 
 
 def finish(r, *refs):
-    out_in, ing_in, res, out, ing, gq, gk, gv, go, gu, gd, gg1, gs1, gg2, gs2, gbu, gbd, sems = refs
-    copies = [pltpu.make_async_copy(out_in, out, sems.at[0]), pltpu.make_async_copy(ing_in, ing, sems.at[1])]
-    for copy in copies:
-        copy.start()
+    out_in, ing_in, res, out, ing, gq, gk, gv, go, gu, gd, gg1, gs1, gg2, gs2, gbu, gbd = refs
+    out[...] = out_in[...]
+    ing[...] = ing_in[...]
     D = res.shape[2]
     me = lax.axis_index("wide")
     for ref, at in ((gq, WQ), (gk, WK), (gv, WV), (go, WO)):
@@ -548,8 +547,6 @@
         row = jnp.where((me * 4 * r) // D == c, tile[5 + c : 6 + c, :], row)
     row = jnp.broadcast_to(row, (8, D))
     gbu[...] = pltpu.roll(row, lax.rem(D - lax.rem(me * 4 * r, D), D), axis=1)[0:1, 0 : 4 * r]
-    for copy in copies:
-        copy.wait()
 
 
 def on_device(sizes, *args):
@@ -560,7 +557,6 @@
     rp = max(r, 16)
     vm = pl.BlockSpec(memory_space=pltpu.VMEM)
     sm = pl.BlockSpec(memory_space=pltpu.SMEM)
-    hbm = pl.BlockSpec(memory_space=pl.ANY)
     inputs = dict(
         tok=tokens[0], cot=cot[0], lens=lengths, cnts=counts, wq=wq, wk=wk, wv=wv, wo=wo.T, up=wu, down=wd.T,
         g1=g1[None], s1=s1[None], g2=g2[None], s2=s2[None], bu=bu[None], bd=bd[None],
@@ -590,9 +586,8 @@
             f(r, D), f(r, D), f(r, D), f(r, D), f(r, 4 * D), f(r, 4 * D),
             f(1, r), f(1, r), f(1, r), f(1, r), f(1, 4 * r), f(1, r),
         ),
-        in_specs=[hbm, hbm, vm],
-        out_specs=(hbm, hbm) + (vm,) * 12,
-        scratch_shapes=[pltpu.SemaphoreType.DMA((2,))],
+        in_specs=[vm] * 3,
+        out_specs=(vm,) * 14,
         name="finish",
     )(out, ing, res)
     return (out[None], ing[None], gq, gk, gv, go.T, gu, gd.T, gg1[0], gs1[0], gg2[0], gs2[0], gbu[0], gbd[0])

time: 118 us -> 85.7 us (0.73)
  Pallas kernels: 116 us -> 83.9 us
    pallas_call x1, Pallas kernels: 34.5 us -> 2.35 us  [on_device(): pl.pallas_call(functools.partial(finish, r), out_shape=(jax.ShapeDtypeStr...]
where the time goes in v2:
time: 85.7 us; the launch traced here: 84.7 us
  Pallas kernels  83.9 us (98%)
    pallas_call x1, Pallas kernels, on_device(): pl.pallas_call(functools.partial(body, names, line, plane, r), out_shape=...  81.5 us
    pallas_call x1, Pallas kernels, on_device(): pl.pallas_call(functools.partial(finish, r), out_shape=(jax.ShapeDtypeStr...  2.35 us

profile of v2, /device:TPU:0, one launch (start us, length us, event | category | flops | bytes accessed | tf_op | source)
XLA Modules:
  0.0 84.7 jit_solution(17840589471689323005)
XLA Ops:
  0.7 81.5 %loop_block.1 = (bf16[1024,256]{1,0:T(8,128)(2,1)}, bf16[1024,256]{1,0:T(8,128)(2,1)}, f32[14,16,256]{2,1,0:T(8,128)}) custom-call(bf16[1024,256]{1,0:T(8,128)(2,1)} %bitcast.20, bf16[1024,256]{1,0:T(8,128)(2,1)} %bitcast.21, s32[1,20]{1,0:T(1,128)} %refs_2_.1, s32[1,20]{1,0:T(1,128)} %refs_3_.1, bf16[16,256]{1,0:T(8,128)(2,1)} %refs_4_.1, ...), custom_call_target="tpu_custom_call" | custom-call | tf_op jit(solution)/shard_map/loop_block/pallas_call | solution.py:566
  82.2 2.3 %finish.1 = (bf16[1024,256]{1,0:T(8,128)(2,1)}, bf16[1024,256]{1,0:T(8,128)(2,1)}, f32[16,256]{1,0:T(8,128)}, f32[16,256]{1,0:T(8,128)}, f32[16,256]{1,0:T(8,128...) custom-call(bf16[1024,256]{1,0:T(8,128)(2,1)} %get-tuple-element.31., ...), custom_call_target="tpu_custom_call" | custom-call | tf_op jit(solution)/shard_map/finish/pallas_call | solution.py:582

commit v3 on v2

--- a/solution.py
+++ b/solution.py
@@ -13,7 +13,6 @@
 HEADS = 4
 NORM_EPS = 1e-05
 MASK_FILL = -1e30
-C = 256
 QB = 128
 NN = (((1,), (0,)), ((), ()))
 NT = (((1,), (1,)), ((), ()))
@@ -75,57 +74,10 @@
         copy.wait_send()
 
 
-def body(names, line, plane, r, *refs):
-    s = dict(zip(names, refs))
-    tok, cot, lens, cnts = s["tok"], s["cot"], s["lens"], s["cnts"]
-    out, ing, res = s["out"], s["ing"], s["res"]
-    wb, G, gs, small = s["wb"], s["G"], s["gs"], s["small"]
-    gb = s.get("gb", wb)
-    S, D = tok.shape
+def layout(s):
+    lens, cnts, G, gs = s["lens"], s["cnts"], s["G"], s["gs"]
+    S, D = s["tok"].shape
     nb = S // QB
-    n = line * plane
-    rp = wb.shape[3]
-    x = Exchange(line, plane)
-    core, me = x.core, x.me
-
-    barrier = pltpu.get_barrier_semaphore()
-    pl.semaphore_signal(barrier, inc=1, device_id=x.sibling(), device_id_type=MESH)
-    for k in range(1, n):
-        pl.semaphore_signal(
-            barrier,
-            inc=1,
-            device_id={"dp": core, "wide": lax.rem(me + k, n)},
-            device_id_type=MESH,
-        )
-
-    lanes = lax.broadcasted_iota(jnp.int32, (16, D), 1)
-    rows16 = lax.broadcasted_iota(jnp.int32, (16, D), 0)
-    tile = s["tile"]
-    tile[...] = jnp.zeros((16, D), F32)
-    for i, key in enumerate(("g1", "s1", "g2", "s2", "bd")):
-        tile[i : i + 1, 0:r] = s[key][...].astype(F32)
-    own = pltpu.roll(tile[...], me * r, axis=1)
-    tile[0:1, 0 : 4 * r] = s["bu"][...].astype(F32)
-    ups = jnp.broadcast_to(tile[0:1, :], (16, D))
-    ups = jnp.where((lanes < 4 * r) & (rows16 == 5 + (me * 4 * r) // D), ups, 0.0)
-    small_own = jnp.where(rows16 < 5, own, pltpu.roll(ups, lax.rem(me * 4 * r, D), axis=1)).astype(BF)
-    first = jnp.where(core == 0, 1.0, 0.0).astype(BF)
-    second = jnp.where(core == 0, 0.0, 1.0).astype(BF)
-
-    def pad(v):
-        return v if rp == r else jnp.concatenate([v.astype(F32), jnp.zeros((rp - r, D), F32)], axis=0).astype(BF)
-
-    up = [pad(s["up"][:, c * D : (c + 1) * D]) for c in range(4)]
-    down = [pad(s["down"][:, c * D : (c + 1) * D]) for c in range(4)]
-    q_own, k_own, v_own, o_own = (pad(s[key][...]) for key in ("wq", "wk", "wv", "wo"))
-    for (base, half), parts in (
-        (GROUP_A, ((small_own, k_own), (q_own, v_own))),
-        (GROUP_B, ((o_own, up[2]), (up[0], up[3]), (up[1], up[3]))),
-        (GROUP_C, ((down[0], down[2]), (down[1], down[3]))),
-    ):
-        for i, (of_first, of_second) in enumerate(parts):
-            wb[base + half * core + i, x.a, x.p] = of_first * first + of_second * second
-
     slot = lax.broadcasted_iota(jnp.int32, (nb, QB), 0) * QB + lax.broadcasted_iota(jnp.int32, (nb, QB), 1)
     end = jnp.int32(0)
     start_of = jnp.zeros((nb, QB), jnp.int32)
@@ -147,68 +99,18 @@
         s["act"][pl.ds(b * QB, QB), :] = jnp.broadcast_to(
             jnp.where(loops_t[:, b : b + 1] > 1, 1.0, 0.0), (QB, 128)
         )
-    lane_head = lax.broadcasted_iota(jnp.int32, (1, D), 1) // (D // HEADS)
-    hm = [jnp.where(lane_head == h, 1.0, 0.0).astype(BF) for h in range(HEADS)]
     for t in range(2):
         s["k"][t, 0:QB, :] = jnp.zeros((QB, D), BF)
         s["v"][t, 0:QB, :] = jnp.zeros((QB, D), BF)
     G[...] = jnp.zeros(G.shape, F32)
     gs[...] = jnp.zeros(gs.shape, F32)
 
-    pl.semaphore_wait(barrier, n)
-
-    def mine(group, buf=wb):
-        base, half = group
-        return buf.at[pl.ds(base + half * core, half)]
-
-    sem = {key: (s["send_" + key], s["recv_" + key]) for key in SEMS(line, plane)}
-    to_a = [
-        send(mine(GROUP_A).at[:, x.a, x.p], mine(GROUP_A).at[:, x.a, x.p], sem["a"], k - 1,
-             {"dp": core, "wide": lax.rem(me + k, n)})
-        for k in range(1, n)
-    ]
-    to_b = [
-        send(mine(GROUP_B).at[:, x.a, x.p], mine(GROUP_B).at[:, x.a, x.p], sem["b1"], k - 1,
-             x.chip(x.along(k), x.p))
-        for k in range(1, line)
-    ]
-    to_c = [
-        send(mine(GROUP_C).at[:, x.a, x.p], mine(GROUP_C).at[:, x.a, x.p], sem["c1"], k - 1,
-             x.chip(x.a, x.across(k)))
-        for k in range(1, plane)
-    ]
-    arrived(to_a)
-    share_a = [send(mine(GROUP_A), mine(GROUP_A), sem["sib"], 0, x.sibling())]
-    arrived(to_b)
-    to_b2 = [
-        send(mine(GROUP_B).at[:, :, x.p], mine(GROUP_B).at[:, :, x.p], sem["b2"], k - 1,
-             x.chip(x.a, x.across(k)))
-        for k in range(1, plane)
-    ]
-    arrived(to_c)
-    to_c2 = [
-        send(mine(GROUP_C).at[:, x.a], mine(GROUP_C).at[:, x.a], sem["c2"], k - 1,
-             x.chip(x.along(k), x.p))
-        for k in range(1, line)
-    ]
-    arrived(share_a)
-    whole_small = wb[SMALL].reshape(n, rp, D).astype(F32)
-    small[...] = jnp.sum(whole_small, axis=0)[0:16]
-
-    def W(i):
-        return wb[i].reshape(D, D) if rp == r else s["wf"][i]
-
-    def places():
-        row = lax.broadcasted_iota(jnp.int32, (D, n * rp), 0)
-        place = lax.broadcasted_iota(jnp.int32, (D, n * rp), 1)
-        return jnp.where(place == (row // r) * rp + lax.rem(row, r), 1.0, 0.0).astype(BF)
-
-    def unpack(base, count):
-        if rp != r:
-
-            @pl.loop(base, base + count)
-            def _(i):
-                s["wf"][i] = dot(places(), wb[i].reshape(n * rp, D)).astype(BF)
+
+def block(s, W, C):
+    tok, cot, out, ing, small, G, gs = (s[key] for key in ("tok", "cot", "out", "ing", "small", "G", "gs"))
+    D = tok.shape[1]
+    lane_head = lax.broadcasted_iota(jnp.int32, (1, D), 1) // (D // HEADS)
+    hm = [jnp.where(lane_head == h, 1.0, 0.0).astype(BF) for h in range(HEADS)]
 
     def wide(v):
         return jnp.concatenate([v, v], axis=1)
@@ -352,12 +254,130 @@
         else:
             ing[rows, :] = (s["bi"][rows, :] + 2.0 * bm).astype(BF)
 
-    chunks = S // C
+    return forward_attention, forward_hidden, backward_hidden, backward_attention
+
+
+def body(names, line, plane, r, *refs):
+    s = dict(zip(names, refs))
+    res, wb, G, gs, small = s["res"], s["wb"], s["G"], s["gs"], s["small"]
+    gb = s.get("gb", wb)
+    S, D = s["tok"].shape
+    n = line * plane
+    rp = wb.shape[3]
+    x = Exchange(line, plane)
+    core, me = x.core, x.me
+
+    barrier = pltpu.get_barrier_semaphore()
+    pl.semaphore_signal(barrier, inc=1, device_id=x.sibling(), device_id_type=MESH)
+    for k in range(1, n):
+        pl.semaphore_signal(
+            barrier,
+            inc=1,
+            device_id={"dp": core, "wide": lax.rem(me + k, n)},
+            device_id_type=MESH,
+        )
+
+    lanes = lax.broadcasted_iota(jnp.int32, (16, D), 1)
+    rows16 = lax.broadcasted_iota(jnp.int32, (16, D), 0)
+    tile = s["tile"]
+    tile[...] = jnp.zeros((16, D), F32)
+    for i, key in enumerate(("g1", "s1", "g2", "s2", "bd")):
+        tile[i : i + 1, 0:r] = s[key][...].astype(F32)
+    own = pltpu.roll(tile[...], me * r, axis=1)
+    tile[0:1, 0 : 4 * r] = s["bu"][...].astype(F32)
+    ups = jnp.broadcast_to(tile[0:1, :], (16, D))
+    ups = jnp.where((lanes < 4 * r) & (rows16 == 5 + (me * 4 * r) // D), ups, 0.0)
+    small_own = jnp.where(rows16 < 5, own, pltpu.roll(ups, lax.rem(me * 4 * r, D), axis=1)).astype(BF)
+    first = jnp.where(core == 0, 1.0, 0.0).astype(BF)
+    second = jnp.where(core == 0, 0.0, 1.0).astype(BF)
+
+    def pad(v):
+        return v if rp == r else jnp.concatenate([v.astype(F32), jnp.zeros((rp - r, D), F32)], axis=0).astype(BF)
+
+    up = [pad(s["up"][:, c * D : (c + 1) * D]) for c in range(4)]
+    down = [pad(s["down"][:, c * D : (c + 1) * D]) for c in range(4)]
+    q_own, k_own, v_own, o_own = (pad(s[key][...]) for key in ("wq", "wk", "wv", "wo"))
+    for (base, half), parts in (
+        (GROUP_A, ((small_own, k_own), (q_own, v_own))),
+        (GROUP_B, ((o_own, up[2]), (up[0], up[3]), (up[1], up[3]))),
+        (GROUP_C, ((down[0], down[2]), (down[1], down[3]))),
+    ):
+        for i, (of_first, of_second) in enumerate(parts):
+            wb[base + half * core + i, x.a, x.p] = of_first * first + of_second * second
+
+    layout(s)
+
+    pl.semaphore_wait(barrier, n)
+
+    def mine(group, buf=wb):
+        base, half = group
+        return buf.at[pl.ds(base + half * core, half)]
+
+    sem = {key: (s["send_" + key], s["recv_" + key]) for key in SEMS(line, plane)}
+    to_a = [
+        send(mine(GROUP_A).at[:, x.a, x.p], mine(GROUP_A).at[:, x.a, x.p], sem["a"], k - 1,
+             {"dp": core, "wide": lax.rem(me + k, n)})
+        for k in range(1, n)
+    ]
+    to_b = [
+        send(mine(GROUP_B).at[:, x.a, x.p], mine(GROUP_B).at[:, x.a, x.p], sem["b1"], k - 1,
+             x.chip(x.along(k), x.p))
+        for k in range(1, line)
+    ]
+    to_c = [
+        send(mine(GROUP_C).at[:, x.a, x.p], mine(GROUP_C).at[:, x.a, x.p], sem["c1"], k - 1,
+             x.chip(x.a, x.across(k)))
+        for k in range(1, plane)
+    ]
+    arrived(to_a)
+    share_a = [send(mine(GROUP_A), mine(GROUP_A), sem["sib"], 0, x.sibling())]
+    arrived(to_b)
+    to_b2 = [
+        send(mine(GROUP_B).at[:, :, x.p], mine(GROUP_B).at[:, :, x.p], sem["b2"], k - 1,
+             x.chip(x.a, x.across(k)))
+        for k in range(1, plane)
+    ]
+    arrived(to_c)
+    to_c2 = [
+        send(mine(GROUP_C).at[:, x.a], mine(GROUP_C).at[:, x.a], sem["c2"], k - 1,
+             x.chip(x.along(k), x.p))
+        for k in range(1, line)
+    ]
+    arrived(share_a)
+    whole_small = wb[SMALL].reshape(n, rp, D).astype(F32)
+    small[...] = jnp.sum(whole_small, axis=0)[0:16]
+
+    def W(i):
+        return wb[i].reshape(D, D) if rp == r else s["wf"][i]
+
+    def places():
+        row = lax.broadcasted_iota(jnp.int32, (D, n * rp), 0)
+        place = lax.broadcasted_iota(jnp.int32, (D, n * rp), 1)
+        return jnp.where(place == (row // r) * rp + lax.rem(row, r), 1.0, 0.0).astype(BF)
+
+    def unpack(base, count):
+        if rp != r:
+
+            @pl.loop(base, base + count)
+            def _(i):
+                s["wf"][i] = dot(places(), wb[i].reshape(n * rp, D)).astype(BF)
+
+    C = s["dq"].shape[0]
+    forward_attention, forward_hidden, backward_hidden, backward_attention = block(s, W, C)
+
+    def chunks(*steps):
+        def one(i):
+            for step, t in steps:
+                step(t, S // C - 1 - i if step in (backward_hidden, backward_attention) else i)
+
+        if S == C:
+            one(0)
+        else:
+            pl.loop(0, S // C)(one)
+
     unpack(WQ, 3)
 
-    @pl.loop(0, chunks)
-    def _(i):
-        forward_attention(0, i)
+    chunks((forward_attention, 0))
 
     arrived(to_b2)
     share_b = [send(mine(GROUP_B), mine(GROUP_B), sem["sib"], 1, x.sibling())]
@@ -367,26 +387,14 @@
     unpack(WO, 5)
     unpack(WD, 4)
 
-    @pl.loop(0, chunks)
-    def _(i):
-        forward_hidden(0, i)
-
-    @pl.loop(0, chunks)
-    def _(i):
-        forward_attention(1, i)
-        forward_hidden(1, i)
+    chunks((forward_hidden, 0))
+    chunks((forward_attention, 1), (forward_hidden, 1))
 
     s["dk"][...] = jnp.zeros(s["dk"].shape, F32)
     s["dv"][...] = jnp.zeros(s["dv"].shape, F32)
 
-    @pl.loop(0, chunks)
-    def _(i):
-        backward_hidden(1, chunks - 1 - i)
-        backward_attention(1, chunks - 1 - i)
-
-    @pl.loop(0, chunks)
-    def _(i):
-        backward_hidden(0, chunks - 1 - i)
+    chunks((backward_hidden, 1), (backward_attention, 1))
+    chunks((backward_hidden, 0))
 
     def stage(base, count):
         @pl.loop(base, base + count)
@@ -424,7 +432,6 @@
 
     s["dk"][...] = jnp.zeros(s["dk"].shape, F32)
     s["dv"][...] = jnp.zeros(s["dv"].shape, F32)
-    backward_attention(0, chunks - 1)
     add_swapped(swap_b, GROUP_B, s["inb"])
     from_b = [
         send(mine(GROUP_B, gb).at[:, :, x.across(k)], s["inb1"].at[k - 1], sem["rb1"], k - 1,
@@ -437,8 +444,10 @@
              x.chip(x.along(k), x.p))
         for k in range(1, line)
     ]
-    for i in range(chunks - 2, 0, -1):
-        backward_attention(0, i)
+    chunks((backward_attention, 0))
+    stage(WQ, 3)
+    gb[SMALL] = jnp.broadcast_to(gs[...].astype(BF)[None, None], (line, plane, 16, D))
+    swap_a = swap(GROUP_A, s["ina"], 0)
     arrived(from_b)
     sum_b = mine(GROUP_B, gb)[:, :, x.p].astype(F32)
     for k in range(1, plane):
@@ -457,10 +466,14 @@
         send(s["sumc"].at[:, x.across(k)], s["inc2"].at[k - 1], sem["rc2"], k - 1, x.chip(x.a, x.across(k)))
         for k in range(1, plane)
     ]
-    backward_attention(0, 0)
-    stage(WQ, 3)
-    gb[SMALL] = jnp.broadcast_to(gs[...].astype(BF)[None, None], (line, plane, 16, D))
-    swap_a = swap(GROUP_A, s["ina"], 0)
+    add_swapped(swap_a, GROUP_A, s["ina"])
+    from_a = []
+    for k in range(1, n):
+        to = lax.rem(me + k, n)
+        from_a.append(
+            send(mine(GROUP_A, gb).at[:, to // plane, lax.rem(to, plane)], s["ina1"].at[k - 1], sem["ra"], k - 1,
+                 {"dp": core, "wide": to})
+        )
     arrived(from_b2)
     total = s["sumb"][:, x.a].astype(F32)
     for k in range(1, line):
@@ -471,14 +484,6 @@
     for k in range(1, plane):
         total = total + s["inc2"][k - 1].astype(F32)
     done_c = finished(GROUP_C, 2, total)
-    add_swapped(swap_a, GROUP_A, s["ina"])
-    from_a = []
-    for k in range(1, n):
-        to = lax.rem(me + k, n)
-        from_a.append(
-            send(mine(GROUP_A, gb).at[:, to // plane, lax.rem(to, plane)], s["ina1"].at[k - 1], sem["ra"], k - 1,
-                 {"dp": core, "wide": to})
-        )
     arrived(from_a)
     total = mine(GROUP_A, gb)[:, x.a, x.p].astype(F32)
     for k in range(1, n):
@@ -500,6 +505,7 @@
 def scratch(S, D, line, plane, rp):
     nb, n = S // QB, line * plane
     V = pltpu.VMEM
+    C = S if D // n == rp else 256
     shapes = dict(
         tile=V((16, D), F32), small=V((16, D), F32),
         wb=V((SLABS, line, plane, rp, D), BF),

time: 85.7 us -> 66.9 us (0.78)
  Pallas kernels: 83.9 us -> 65.6 us
    pallas_call x1, Pallas kernels: 81.5 us -> 63.2 us  [on_device(): pl.pallas_call(functools.partial(body, names, line, plane, r), out_shape=...]
where the time goes in v3:
time: 66.9 us; the launch traced here: 66.4 us
  Pallas kernels  65.6 us (98%)
  between operations  0.84 us (1%)
    pallas_call x1, Pallas kernels, on_device(): pl.pallas_call(functools.partial(body, names, line, plane, r), out_shape=...  63.2 us
    pallas_call x1, Pallas kernels, on_device(): pl.pallas_call(functools.partial(finish, r), out_shape=(jax.ShapeDtypeStr...  2.35 us

profile of v3, /device:TPU:0, one launch (start us, length us, event | category | flops | bytes accessed | tf_op | source)
XLA Modules:
  0.0 66.4 jit_solution(1556586706572785982)
XLA Ops:
  0.7 63.2 %loop_block.1 = (bf16[1024,256]{1,0:T(8,128)(2,1)}, bf16[1024,256]{1,0:T(8,128)(2,1)}, f32[14,16,256]{2,1,0:T(8,128)}) custom-call(bf16[1024,256]{1,0:T(8,128)(2,1)} %bitcast.20, bf16[1024,256]{1,0:T(8,128)(2,1)} %bitcast.21, s32[1,20]{1,0:T(1,128)} %refs_2_.1, s32[1,20]{1,0:T(1,128)} %refs_3_.1, bf16[16,256]{1,0:T(8,128)(2,1)} %refs_4_.1, ...), custom_call_target="tpu_custom_call" | custom-call | tf_op jit(solution)/shard_map/loop_block/pallas_call | solution.py:572
  63.9 2.3 %finish.1 = (bf16[1024,256]{1,0:T(8,128)(2,1)}, bf16[1024,256]{1,0:T(8,128)(2,1)}, f32[16,256]{1,0:T(8,128)}, f32[16,256]{1,0:T(8,128)}, f32[16,256]{1,0:T(8,128...) custom-call(bf16[1024,256]{1,0:T(8,128)(2,1)} %get-tuple-element.31., ...), custom_call_target="tpu_custom_call" | custom-call | tf_op jit(solution)/shard_map/finish/pallas_call | solution.py:588

commit v4 on v3

v4 whole, which is shorter than its diff:
```python
import functools
import math

import jax
import jax.numpy as jnp
from jax import lax
from jax.experimental import pallas as pl
from jax.experimental.pallas import tpu as pltpu
from jax.sharding import PartitionSpec as P

F32, BF = jnp.float32, jnp.bfloat16
MESH = pl.DeviceIdType.MESH
HEADS = 4
NORM_EPS = 1e-05
MASK_FILL = -1e30
QB = 128
NN = (((1,), (0,)), ((), ()))
NT = (((1,), (1,)), ((), ()))
TN = (((0,), (0,)), ((), ()))
C0 = math.sqrt(2 / math.pi)
C1 = C0 * 0.044715

SMALL, WQ, WK, WV, WO, WU, WD = 0, 1, 2, 3, 4, 5, 10
SLABS = 14
GROUP_A, GROUP_B, GROUP_C = (0, 2), (4, 3), (10, 2)


def dot(a, b, dims=NN):
    return lax.dot_general(a, b, dims, preferred_element_type=F32)


FETCHED = ("lens", "cnts", "wq", "wk", "wv", "wo", "up", "down", "g1", "s1", "g2", "s2", "bu", "bd")


class Exchange:
    def __init__(self, line, plane):
        self.line, self.plane = line, plane
        self.n = line * plane
        self.core = lax.axis_index("dp")
        self.me = lax.axis_index("wide")
        self.a = self.me // plane
        self.p = self.me % plane

    def chip(self, a, p):
        return {"dp": self.core, "wide": a * self.plane + p}

    def sibling(self):
        return {"dp": 1 - self.core, "wide": self.me}

    def along(self, step):
        return lax.rem(self.a + step, self.line)

    def across(self, step):
        return lax.rem(self.p + step, self.plane)


class Copies:
    def __init__(self, sems, k, size):
        self.send_sem, self.recv_sem, self.size = sems[0].at[k], sems[1].at[k], size

    def start(self, src, dst, device):
        pltpu.make_async_remote_copy(
            src_ref=src,
            dst_ref=dst,
            send_sem=self.send_sem,
            recv_sem=self.recv_sem,
            device_id=device,
            device_id_type=MESH,
        ).start()

    def arrived(self):
        pltpu.make_async_copy(self.size, self.size, self.recv_sem).wait()

    def left(self):
        pltpu.make_async_copy(self.size, self.size, self.send_sem).wait()


def arrived(*copies):
    for copy in copies:
        copy.arrived()


def left(*copies):
    for copy in copies:
        copy.left()


def layout(s):
    lens, cnts, G, gs = s["lens"], s["cnts"], s["G"], s["gs"]
    S, D = s["tok"].shape
    nb = S // QB
    slot = lax.broadcasted_iota(jnp.int32, (nb, QB), 0) * QB + lax.broadcasted_iota(jnp.int32, (nb, QB), 1)
    end = jnp.int32(0)
    start_of = jnp.zeros((nb, QB), jnp.int32)
    loops_of = jnp.zeros((nb, QB), jnp.int32)
    for j in range(lens.shape[1]):
        inside = slot >= end
        start_of = jnp.where(inside, end, start_of)
        loops_of = jnp.where(inside, cnts[0, j], loops_of)
        end = end + lens[0, j]
    start_t = jnp.transpose(start_of.astype(F32))
    loops_t = jnp.transpose(loops_of.astype(F32))
    kk = lax.broadcasted_iota(jnp.int32, (QB, 2 * QB), 1).astype(F32)
    qq = lax.broadcasted_iota(jnp.int32, (QB, 2 * QB), 0).astype(F32)
    for b in range(nb):
        ok = (kk >= start_t[:, b : b + 1] - (b - 1) * QB) & (kk <= qq + QB)
        if b == 0:
            ok = ok & (kk >= QB)
        s["mask"][b] = jnp.where(ok, 0.0, MASK_FILL)
        s["act"][pl.ds(b * QB, QB), :] = jnp.broadcast_to(
            jnp.where(loops_t[:, b : b + 1] > 1, 1.0, 0.0), (QB, 128)
        )
    for t in range(2):
        s["k"][t, 0:QB, :] = jnp.zeros((QB, D), BF)
        s["v"][t, 0:QB, :] = jnp.zeros((QB, D), BF)
    G[...] = jnp.zeros(G.shape, F32)
    gs[...] = jnp.zeros(gs.shape, F32)


def no_keys_ahead(s):
    for key in ("dk", "dv"):
        ref = s[key]
        ref[pl.ds(ref.shape[0] - QB, QB), :] = jnp.zeros((QB, ref.shape[1]), F32)


def block(s, W, C):
    tok, cot, out, ing, small, G, gs = (s[key] for key in ("tok", "cot", "out", "ing", "small", "G", "gs"))
    D = tok.shape[1]
    scale = (D // HEADS) ** -0.5
    lane_head = lax.broadcasted_iota(jnp.int32, (1, D), 1) // (D // HEADS)
    hm = [jnp.where(lane_head == h, 1.0, 0.0).astype(BF) for h in range(HEADS)]

    def wide(v):
        return jnp.concatenate([v, v], axis=1)

    def by_head(v):
        return jnp.concatenate([v * hm[h] for h in range(HEADS)], axis=0)

    def of_heads(v):
        own = v[0:QB]
        for h in range(1, HEADS):
            own = jnp.where(lane_head == h, v[h * QB : (h + 1) * QB], own)
        return own

    def block_rows(b):
        at = lambda k, size: pl.ds(pl.multiple_of(k * QB, QB), size)
        return at(b, 2 * QB), at(b, QB), at(b + 1, QB)

    def normalized(v):
        mean = jnp.mean(v, axis=1, keepdims=True)
        cen = v - mean
        var = jnp.mean(cen * cen, axis=1, keepdims=True)
        rstd = lax.rsqrt(var + NORM_EPS)
        return cen * rstd, jnp.broadcast_to(rstd, (C, 128))

    def add(ref, at, t, value):
        if t == 1 and C == tok.shape[0]:
            ref[at] = value
        else:
            ref[at] += value

    def forward_mixed(t, i):
        rows = pl.ds(pl.multiple_of(i * C, C), C)
        tk = tok[rows, :].astype(F32)
        mixed = tk + tk if t == 0 else s["state"][rows, :] + tk
        s["mixed"][rows, :] = mixed
        s["z1"][t, rows, :], s["r1"][t, rows, :] = normalized(mixed)

    def forward_attention(t, i):
        r0 = pl.multiple_of(i * C, C)
        rows = pl.ds(r0, C)
        n1 = (s["z1"][t, rows, :] * small[0:1, :] + small[1:2, :]).astype(BF)
        s["n1"][t, rows, :] = n1
        q = dot(n1, W(WQ)).astype(BF)
        s["q"][t, rows, :] = q
        s["k"][t, pl.ds(r0 + QB, C), :] = dot(n1, W(WK)).astype(BF)
        s["v"][t, pl.ds(r0 + QB, C), :] = dot(n1, W(WV)).astype(BF)
        for u in range(C // QB):
            b = i * (C // QB) + u
            win = pl.ds(pl.multiple_of(b * QB, QB), 2 * QB)
            kw, vw = s["k"][t, win, :], s["v"][t, win, :]
            qb = q[u * QB : (u + 1) * QB]
            sc = dot(by_head(qb), kw, NT)
            mask = s["mask"][b]
            ps = []
            for h in range(HEADS):
                e = sc[h * QB : (h + 1) * QB] * scale + mask
                e = jnp.exp(e - jnp.max(e, axis=1, keepdims=True))
                ps.append((e * (1.0 / jnp.sum(e, axis=1, keepdims=True))).astype(BF))
            p = jnp.concatenate(ps, axis=0)
            s["p"][t, b] = p
            s["at"][t, pl.ds(pl.multiple_of(b * QB, QB), QB), :] = of_heads(dot(p, vw)).astype(BF)

    def forward_hidden(t, i):
        rows = pl.ds(pl.multiple_of(i * C, C), C)
        resid = s["mixed"][rows, :] + dot(s["at"][t, rows, :], W(WO), NT)
        z2, s["r2"][t, rows, :] = normalized(resid)
        s["z2"][t, rows, :] = z2
        n2 = (z2 * small[2:3, :] + small[3:4, :]).astype(BF)
        s["n2"][t, rows, :] = n2
        acc = resid + small[4:5, :]
        for c in range(4):
            hp = dot(n2, W(WU + c)) + small[5 + c : 6 + c, :]
            v2 = hp * hp
            th = jnp.tanh(hp * (C1 * v2 + C0))
            pr = 0.5 * th + 0.5
            g = hp * pr
            d = pr + g * (1.0 - pr) * ((6 * C1) * v2 + (2 * C0))
            g = g.astype(BF)
            s["h"][t, c, rows, :] = g
            s["d"][t, c, rows, :] = d.astype(BF)
            acc = acc + dot(g, W(WD + c), NT)
        if t == 0:
            s["state"][rows, :] = acc
        else:
            act = wide(s["act"][rows, :])
            out[rows, :] = jnp.where(act > 0, acc, s["state"][rows, :]).astype(BF)

    def norm_bwd(t, dn, g, z, rstd, gi):
        e = dn * g
        add(gs, slice(gi, gi + 1), t, jnp.sum(dn * z, axis=0, keepdims=True))
        add(gs, slice(gi + 1, gi + 2), t, jnp.sum(dn, axis=0, keepdims=True))
        m1 = jnp.mean(e, axis=1, keepdims=True)
        m2 = jnp.mean(e * z, axis=1, keepdims=True)
        return wide(rstd) * (e - m1 - z * m2)

    def back_renewed(t, rows):
        if t == 0:
            return s["state"][rows, :]
        return jnp.where(wide(s["act"][rows, :]) > 0, cot[rows, :].astype(F32), 0.0)

    def backward_hidden(t, i):
        rows = pl.ds(pl.multiple_of(i * C, C), C)
        br = back_renewed(t, rows)
        add(gs, slice(4, 5), t, jnp.sum(br, axis=0, keepdims=True))
        b2 = br.astype(BF)
        b2t = b2.T
        n2t = s["n2"][t, rows, :].T
        dn2 = jnp.zeros((C, D), F32)
        for c in range(4):
            add(G, WD + c, t, dot(b2t, s["h"][t, c, rows, :]))
            dp = s["d"][t, c, rows, :].astype(F32) * dot(b2, W(WD + c))
            add(gs, slice(5 + c, 6 + c), t, jnp.sum(dp, axis=0, keepdims=True))
            dp = dp.astype(BF)
            add(G, WU + c, t, dot(n2t, dp))
            dn2 = dn2 + dot(dp, W(WU + c), NT)
        bres = br + norm_bwd(t, dn2, small[2:3, :], s["z2"][t, rows, :], s["r2"][t, rows, :], 2)
        s["bres"][rows, :] = bres
        b1 = bres.astype(BF)
        add(G, WO, t, dot(b1.T, s["at"][t, rows, :]))
        s["do"][rows, :] = dot(b1, W(WO)).astype(BF)

    def backward_scores(t, i, blocks):
        for b in reversed(blocks):
            b = i * (C // QB) + b
            win, behind, ahead = block_rows(b)
            kw, vw = s["k"][t, win, :], s["v"][t, win, :]
            qs, dos = by_head(s["q"][t, behind, :]), by_head(s["do"][behind, :])
            p = s["p"][t, b]
            pf = p.astype(F32)
            tt = pf * dot(dos, vw, NT)
            ds = (tt - pf * jnp.sum(tt, axis=1, keepdims=True)).astype(BF)
            s["dq"][behind, :] = (of_heads(dot(ds, kw)) * scale).astype(BF)
            for ref, value in ((s["dv"], dot(p, dos, TN)), (s["dk"], dot(ds, qs, TN))):
                ref[behind, :] = value[0:QB]
                ref[ahead, :] += value[QB:]

    def backward_late(t, i):
        backward_scores(t, i, range(C // QB // 2, C // QB))

    def backward_early(t, i):
        backward_scores(t, i, range(C // QB // 2))
        rows = pl.ds(pl.multiple_of(i * C, C), C)
        own_keys = pl.ds(pl.multiple_of(i * C, C) + QB, C)
        n1t = s["n1"][t, rows, :].T
        add(G, WQ, t, dot(n1t, s["dq"][rows, :]))
        add(G, WK, t, dot(n1t, (s["dk"][own_keys, :] * scale).astype(BF)))
        add(G, WV, t, dot(n1t, s["dv"][own_keys, :].astype(BF)))

    def backward_mixed(t, i):
        r0 = pl.multiple_of(i * C, C)
        rows = pl.ds(r0, C)
        own_keys = pl.ds(r0 + QB, C)
        dn1 = dot(s["dq"][rows, :], W(WQ), NT)
        dn1 = dn1 + dot((s["dk"][own_keys, :] * scale).astype(BF), W(WK), NT)
        dn1 = dn1 + dot(s["dv"][own_keys, :].astype(BF), W(WV), NT)
        back = norm_bwd(t, dn1, small[0:1, :], s["z1"][t, rows, :], s["r1"][t, rows, :], 0)
        bm = s["bres"][rows, :] + back
        if t == 1:
            s["bi"][rows, :] = bm
            s["state"][rows, :] = jnp.where(wide(s["act"][rows, :]) > 0, 0.0, cot[rows, :].astype(F32)) + bm
        else:
            ing[rows, :] = (s["bi"][rows, :] + 2.0 * bm).astype(BF)

    forward = (forward_mixed, forward_attention, forward_hidden)
    return forward, (backward_hidden, backward_late, backward_early, backward_mixed)


def body(names, line, plane, r, *refs):
    s = dict(zip(names, refs))
    res, wb, G, gs, small = s["res"], s["wb"], s["G"], s["gs"], s["small"]
    gb = s.get("gb", wb)
    S, D = s["tok"].shape
    n = line * plane
    rp = wb.shape[3]
    x = Exchange(line, plane)
    core, me = x.core, x.me

    large = s["large"]
    fetch_tok = pltpu.make_async_copy(s["tok_hbm"], s["tok"], large.at[0])
    fetch_cot = pltpu.make_async_copy(s["cot_hbm"], s["cot"], large.at[1])
    store_out = pltpu.make_async_copy(s["out"], s["out_hbm"], large.at[2])
    store_ing = pltpu.make_async_copy(s["ing"], s["ing_hbm"], large.at[3])
    barrier = pltpu.get_barrier_semaphore()
    pl.semaphore_signal(barrier, inc=1, device_id=x.sibling(), device_id_type=MESH)
    for k in range(1, n):
        pl.semaphore_signal(
            barrier,
            inc=1,
            device_id={"dp": core, "wide": lax.rem(me + k, n)},
            device_id_type=MESH,
        )

    fetches = [
        pltpu.make_async_copy(s[key + "_hbm"], s[key], s["fetch"].at[i]) for i, key in enumerate(FETCHED)
    ]
    for copy in (*fetches, fetch_tok, fetch_cot):
        copy.start()
    for copy in fetches:
        copy.wait()

    for k in range(1, plane):
        device = {"dp": 1 - core, "wide": x.chip(x.a, x.across(k))["wide"]}
        pl.semaphore_signal(barrier, inc=1, device_id=device, device_id_type=MESH)

    lanes = lax.broadcasted_iota(jnp.int32, (16, D), 1)
    rows16 = lax.broadcasted_iota(jnp.int32, (16, D), 0)
    tile = s["tile"]
    tile[...] = jnp.zeros((16, D), F32)
    for i, key in enumerate(("g1", "s1", "g2", "s2", "bd")):
        tile[i : i + 1, 0:r] = s[key][...].astype(F32)
    own = pltpu.roll(tile[...], me * r, axis=1)
    tile[0:1, 0 : 4 * r] = s["bu"][...].astype(F32)
    ups = jnp.broadcast_to(tile[0:1, :], (16, D))
    ups = jnp.where((lanes < 4 * r) & (rows16 == 5 + (me * 4 * r) // D), ups, 0.0)
    small_own = jnp.where(rows16 < 5, own, pltpu.roll(ups, lax.rem(me * 4 * r, D), axis=1)).astype(BF)
    first = jnp.where(core == 0, 1.0, 0.0).astype(BF)
    second = jnp.where(core == 0, 0.0, 1.0).astype(BF)

    def pad(v):
        return v if rp == r else jnp.concatenate([v.astype(F32), jnp.zeros((rp - r, D), F32)], axis=0).astype(BF)

    up = [pad(s["up"][:, c * D : (c + 1) * D]) for c in range(4)]
    down = [pad(s["down"][:, c * D : (c + 1) * D]) for c in range(4)]
    q_own, k_own, v_own, o_own = (pad(s[key][...]) for key in ("wq", "wk", "wv", "wo"))
    for (base, half), parts in (
        (GROUP_A, ((small_own, k_own), (q_own, v_own))),
        (GROUP_B, ((o_own, up[2]), (up[0], up[3]), (up[1], up[3]))),
        (GROUP_C, ((down[0], down[2]), (down[1], down[3]))),
    ):
        for i, (of_first, of_second) in enumerate(parts):
            wb[base + half * core + i, x.a, x.p] = of_first * first + of_second * second

    layout(s)

    def W(i):
        return wb[i].reshape(D, D) if rp == r else s["wf"][i]

    def places():
        row = lax.broadcasted_iota(jnp.int32, (D, n * rp), 0)
        place = lax.broadcasted_iota(jnp.int32, (D, n * rp), 1)
        return jnp.where(place == (row // r) * rp + lax.rem(row, r), 1.0, 0.0).astype(BF)

    def unpack(base, count):
        if rp != r:

            @pl.loop(base, base + count)
            def _(i):
                s["wf"][i] = dot(places(), wb[i].reshape(n * rp, D)).astype(BF)

    C = S if rp == r else 256
    forward, backward = block(s, W, C)
    forward_mixed, forward_attention, forward_hidden = forward
    backward_hidden, backward_late, backward_early, backward_mixed = backward

    def chunks(t, *steps):
        def one(i):
            for step in steps:
                step(t, S // C - 1 - i if step in backward else i)

        if S == C:
            one(0)
        else:
            pl.loop(0, S // C)(one)

    fetch_tok.wait()
    chunks(0, forward_mixed)

    def mine(group):
        base, half = group
        return wb.at[pl.ds(base + half * core, half)]

    def start_all(k, size, sends):
        copies = Copies((s["send"], s["recv"]), k, size)
        for send in sends:
            copies.start(*send)
        return copies

    def along_line(k, size, ref, inbox):
        return start_all(k, size, [(ref(x.along(i)), inbox(i), x.chip(x.along(i), x.p)) for i in range(1, line)])

    def across_plane(k, size, ref, inbox):
        return start_all(k, size, [(ref(x.across(i)), inbox(i), x.chip(x.a, x.across(i))) for i in range(1, plane)])

    def to_sibling(k, size, src, dst):
        return start_all(k, size, [(src, dst, x.sibling())])

    def share(k, group):
        return to_sibling(k, mine(group), mine(group), mine(group))

    def bytes_of(group, devices):
        return s["size"].at[pl.ds(0, group[1]), pl.ds(0, devices)]

    pl.semaphore_wait(barrier, n + plane - 1)
    own_b, own_c = (mine(group).at[:, x.a, x.p] for group in (GROUP_B, GROUP_C))
    to_b = along_line(0, bytes_of(GROUP_B, line - 1), lambda _: own_b, lambda _: own_b)
    to_c = along_line(1, bytes_of(GROUP_C, line - 1), lambda _: own_c, lambda _: own_c)
    own_a = mine(GROUP_A).at[:, x.a, x.p]
    everyone = [{"dp": core, "wide": lax.rem(me + k, n)} for k in range(1, n)]
    to_a = start_all(2, bytes_of(GROUP_A, n - 1), [(own_a, own_a, device) for device in everyone])
    arrived(to_b)
    line_b, line_c = (mine(group).at[:, :, x.p] for group in (GROUP_B, GROUP_C))
    to_b2 = across_plane(3, bytes_of(GROUP_B, line * (plane - 1)), lambda _: line_b, lambda _: line_b)
    arrived(to_c)
    to_c2 = across_plane(4, bytes_of(GROUP_C, line * (plane - 1)), lambda _: line_c, lambda _: line_c)
    arrived(to_a)
    share_a = share(5, GROUP_A)
    arrived(share_a)
    small[...] = jnp.sum(wb[SMALL].reshape(n, rp, D).astype(F32), axis=0)[0:16]
    unpack(WQ, 3)
    chunks(0, forward_attention)
    arrived(to_b2)
    share_b = share(6, GROUP_B)
    arrived(to_c2)
    share_c = share(7, GROUP_C)
    arrived(share_b, share_c)
    unpack(WO, 5)
    unpack(WD, 4)
    chunks(0, forward_hidden)
    chunks(1, forward_mixed, forward_attention, forward_hidden)

    store_out.start()
    fetch_cot.wait()
    no_keys_ahead(s)
    chunks(1, *backward)

    def blocks(i):
        if rp == r:
            return G[i].astype(BF).reshape(line, plane, r, D)
        return dot(places(), G[i].astype(BF), TN).astype(BF).reshape(line, plane, rp, D)

    def stage(first_slab, *weights):
        for k, i in enumerate(weights):
            gb[first_slab + k] = blocks(i)

    def kept(ref):
        half = ref.shape[0] // 2
        return ref.at[pl.ds(half * core, half)]

    def swap(k, ref, inbox):
        half = ref.shape[0] // 2
        return to_sibling(k, inbox, ref.at[pl.ds(half * (1 - core), half)], inbox)

    def add_swapped(copies, ref, inbox):
        arrived(copies)
        own = kept(ref)

        def one(i):
            own[i] = (own[i].astype(F32) + inbox[i].astype(F32)).astype(BF)

        pl.loop(0, own.shape[0])(one)

    def total(own, inbox):
        own = own.astype(F32)
        for k in range(inbox.shape[0]):
            own = own + inbox[k].astype(F32)
        return own

    def finished(k, ref, sums):
        part = kept(ref)
        part[...] = sums
        return to_sibling(k, part, part, part)

    def straight(k, ref, inbox):
        sends = []
        for i in range(n - 1):
            to = i + jnp.where(i >= me, 1, 0)
            device = {"dp": core, "wide": to}
            sends.append((kept(ref).at[:, to // plane, lax.rem(to, plane)], inbox.at[me - jnp.where(me > to, 1, 0)], device))
        return start_all(k, inbox, sends)

    def summed(ref, own, inbox):
        ref[...] = total(own, inbox).astype(BF)
        return ref

    left(to_a, to_b, to_c, to_b2, to_c2, share_a, share_b, share_c)
    gb_u, gb_d, gb_q = gb.at[pl.ds(0, 6)], gb.at[pl.ds(6, 4)], s["gq"]
    res_q, res_u, res_d = s["resq"], res.at[pl.ds(0, 6)], res.at[pl.ds(6, 4)]

    chunks(0, backward_hidden)
    stage(6, WD, WD + 1, WD + 2, WD + 3)
    swap_d = swap(8, gb_d, s["ind"])
    stage(0, WO, WU, WU + 1, WU + 2, WU + 3)
    gb[5] = jnp.zeros(gb.shape[1:], BF)
    swap_u = swap(9, gb_u, s["inu"])
    no_keys_ahead(s)
    chunks(0, backward_late)
    add_swapped(swap_d, gb_d, s["ind"])
    from_d = along_line(10, s["in1d"], lambda a: kept(gb_d).at[:, a], lambda i: s["in1d"].at[i - 1])
    add_swapped(swap_u, gb_u, s["inu"])
    from_u = across_plane(11, s["in1u"], lambda p: kept(gb_u).at[:, :, p], lambda i: s["in1u"].at[i - 1])
    chunks(0, backward_early)
    gb_q[0, :, :, :, 0:D] = blocks(WQ)
    gb_q[1, :, :, :, 0:D] = blocks(WK)
    value_blocks = blocks(WV)
    for c in range(2):
        gb_q[c, :, :, :, pl.ds(D, 128)] = value_blocks[:, :, :, 128 * c : 128 * (c + 1)]
    swap_q = swap(15, gb_q, s["inq"])
    chunks(0, backward_mixed)
    store_ing.start()
    vectors = s["vectors"]
    vectors[...] = gs[...].astype(BF)
    near = [{"dp": other, "wide": x.chip(x.a, x.across(i))["wide"]} for other in (core, 1 - core) for i in range(plane)]
    from_v = start_all(23, s["inv"], [(vectors, s["inv"].at[i], device) for i, device in enumerate(near[1:])])
    add_swapped(swap_q, gb_q, s["inq"])
    from_q = straight(16, gb_q, s["intq"])
    arrived(from_d)
    sumd = summed(s["sumd"], kept(gb_d)[:, x.a], s["in1d"])
    from_d2 = across_plane(14, s["in2d"], lambda p: sumd.at[:, p], lambda i: s["in2d"].at[i - 1])
    arrived(from_u)
    sumu = summed(s["sumu"], kept(gb_u)[:, :, x.p], s["in1u"])
    from_u2 = along_line(17, s["in2u"], lambda a: sumu.at[:, a], lambda i: s["in2u"].at[i - 1])
    arrived(from_v)
    sumv = summed(s["sumv"], vectors[...], s["inv"])
    from_v2 = along_line(24, s["in2v"], lambda _: sumv, lambda i: s["in2v"].at[i - 1])
    arrived(from_d2)
    done_d = finished(18, res_d, total(sumd[:, x.p], s["in2d"]))
    arrived(from_u2)
    done_u = finished(20, res_u, total(sumu[:, x.a], s["in2u"]))
    arrived(from_q)
    done_q = finished(21, res_q, total(kept(gb_q)[:, x.a, x.p], s["intq"]))
    arrived(from_v2)
    s["vec"][...] = total(sumv[...], s["in2v"])
    arrived(done_d, done_u, done_q)
    left(swap_d, swap_u, swap_q, from_d, from_d2, from_u, from_u2, from_q, from_v, from_v2)
    left(done_d, done_u, done_q)
    store_out.wait()
    store_ing.wait()


def scratch(S, D, line, plane, rp):
    nb, n = S // QB, line * plane
    V = pltpu.VMEM
    shapes = dict(
        tok=V((S, D), BF), cot=V((S, D), BF), out=V((S, D), BF), ing=V((S, D), BF),
        large=pltpu.SemaphoreType.DMA((4,)), tile=V((16, D), F32), small=V((16, D), F32),
        wb=V((SLABS, line, plane, rp, D), BF),
        G=V((SLABS, D, D), F32), gs=V((16, D), F32),
        gq=V((2, line, plane, rp, D + 128), BF), inq=V((1, line, plane, rp, D + 128), BF),
        intq=V((n - 1, 1, rp, D + 128), BF), size=V((3, n, rp, D), BF),
        vectors=V((16, D), BF), inv=V((2 * plane - 1, 16, D), BF), sumv=V((16, D), BF), in2v=V((line - 1, 16, D), BF),
        inu=V((3, line, plane, rp, D), BF), in1u=V((plane - 1, 3, line, rp, D), BF),
        in2u=V((line - 1, 3, rp, D), BF), sumu=V((3, line, rp, D), BF),
        ind=V((2, line, plane, rp, D), BF), in1d=V((line - 1, 2, plane, rp, D), BF),
        in2d=V((plane - 1, 2, rp, D), BF), sumd=V((2, plane, rp, D), BF),
        mask=V((nb, QB, 2 * QB), F32), act=V((S, 128), F32), state=V((S, D), F32), mixed=V((S, D), F32),
        z1=V((2, S, D), F32), r1=V((2, S, 128), F32), n1=V((2, S, D), BF),
        z2=V((2, S, D), F32), r2=V((2, S, 128), F32), n2=V((2, S, D), BF),
        q=V((2, S, D), BF), k=V((2, S + QB, D), BF), v=V((2, S + QB, D), BF),
        p=V((2, nb, HEADS * QB, 2 * QB), BF), at=V((2, S, D), BF),
        h=V((2, 4, S, D), BF), d=V((2, 4, S, D), BF),
        bres=V((S, D), F32), do=V((S, D), BF),
        dq=V((S, D), BF), dk=V((S + QB, D), F32), dv=V((S + QB, D), F32), bi=V((S, D), F32),
    )
    if D // n != rp:
        shapes["wf"] = V((SLABS, D, D), BF)
    else:
        shapes["gb"] = V((10, line, plane, rp, D), BF)
    shapes["send"] = pltpu.SemaphoreType.DMA((25,))
    shapes["recv"] = pltpu.SemaphoreType.DMA((25,))
    return shapes


def finish(r, *refs):
    out_in, ing_in, res, resq, vec, out, ing, gq, gk, gv, go, gu, gd, gg1, gs1, gg2, gs2, gbu, gbd = refs
    out[...] = out_in[...]
    ing[...] = ing_in[...]
    D = res.shape[2]
    me = lax.axis_index("wide")
    gq[...] = resq[0, 0:r, 0:D]
    gk[...] = resq[1, 0:r, 0:D]
    for c in range(2):
        gv[:, 128 * c : 128 * (c + 1)] = resq[c, 0:r, D:]
    go[...] = res[0, 0:r, :]
    for c in range(4):
        gu[:, c * D : (c + 1) * D] = res[1 + c, 0:r, :]
        gd[:, c * D : (c + 1) * D] = res[6 + c, 0:r, :]
    tile = vec[...]
    own = pltpu.roll(tile, lax.rem(D - me * r, D), axis=1)
    for i, ref in enumerate((gg1, gs1, gg2, gs2, gbd)):
        ref[...] = own[i : i + 1, 0:r]
    row = jnp.zeros((1, D), F32)
    for c in range(4):
        row = jnp.where((me * 4 * r) // D == c, tile[5 + c : 6 + c, :], row)
    row = jnp.broadcast_to(row, (8, D))
    gbu[...] = pltpu.roll(row, lax.rem(D - lax.rem(me * 4 * r, D), D), axis=1)[0:1, 0 : 4 * r]


def on_device(sizes, *args):
    (tokens, lengths, counts, wq, wk, wv, wo, wu, wd, g1, s1, g2, s2, bu, bd, cot) = args
    line, plane = sizes
    S, D = tokens.shape[1:]
    r = wq.shape[0]
    rp = max(r, 16)
    vm = pl.BlockSpec(memory_space=pltpu.VMEM)
    hbm = pl.BlockSpec(memory_space=pl.ANY)
    inputs = dict(
        tok=tokens[0], cot=cot[0], lens=lengths, cnts=counts, wq=wq, wk=wk, wv=wv, wo=wo.T, up=wu, down=wd.T,
        g1=g1[None], s1=s1[None], g2=g2[None], s2=s2[None], bu=bu[None], bd=bd[None],
    )
    shapes = scratch(S, D, line, plane, rp)
    for key in FETCHED:
        space = pltpu.SMEM if key in ("lens", "cnts") else pltpu.VMEM
        shapes[key] = space(inputs[key].shape, inputs[key].dtype)
    shapes["fetch"] = pltpu.SemaphoreType.DMA((len(FETCHED),))
    names = [*(key + "_hbm" for key in inputs), "out_hbm", "ing_hbm", "res", "resq", "vec", *shapes]
    out, ing, res, resq, vec = pl.pallas_call(
        functools.partial(body, names, line, plane, r),
        out_shape=(
            jax.ShapeDtypeStruct((S, D), BF),
            jax.ShapeDtypeStruct((S, D), BF),
            jax.ShapeDtypeStruct((10, rp, D), F32),
            jax.ShapeDtypeStruct((2, rp, D + 128), F32),
            jax.ShapeDtypeStruct((16, D), F32),
        ),
        in_specs=[hbm] * len(inputs),
        out_specs=(hbm, hbm, vm, vm, vm),
        scratch_shapes=list(shapes.values()),
        compiler_params=pltpu.CompilerParams(
            collective_id=0, has_side_effects=True, vmem_limit_bytes=60 * 2**20
        ),
        name="loop_block",
    )(*inputs.values())
    f = lambda *shape: jax.ShapeDtypeStruct(shape, F32)
    out, ing, gq, gk, gv, go, gu, gd, gg1, gs1, gg2, gs2, gbu, gbd = pl.pallas_call(
        functools.partial(finish, r),
        out_shape=(
            jax.ShapeDtypeStruct((S, D), BF), jax.ShapeDtypeStruct((S, D), BF),
            f(r, D), f(r, D), f(r, D), f(r, D), f(r, 4 * D), f(r, 4 * D),
            f(1, r), f(1, r), f(1, r), f(1, r), f(1, 4 * r), f(1, r),
        ),
        in_specs=[vm] * 5,
        out_specs=(vm,) * 14,
        name="finish",
    )(out, ing, res, resq, vec)
    return (out[None], ing[None], gq, gk, gv, go.T, gu, gd.T, gg1[0], gs1[0], gg2[0], gs2[0], gbu[0], gbd[0])


def solution(mesh):
    wide = mesh.shape["wide"]
    line = 4 if wide % 4 == 0 else 1
    rows = P(("dp", "wide"), None, None)
    row = P(("dp", "wide"), None)
    first, second, one = P("wide", None), P(None, "wide"), P("wide")
    weights = (first, first, first, second, first, second)
    return jax.shard_map(
        functools.partial(on_device, (line, wide // line)),
        mesh=mesh,
        in_specs=(rows, row, row, *weights, *(one,) * 6, rows),
        out_specs=(rows, rows, *weights, *(one,) * 6),
        check_vma=False,
    )
```

time: 66.9 us -> 66.4 us (level)
  no operation moved by 1% of the time
where the time goes in v4:
time: 66.4 us; the launch traced here: 66.3 us
  Pallas kernels  65.4 us (98%)
  between operations  0.84 us (1%)
    pallas_call x1, Pallas kernels, on_device(): pl.pallas_call(functools.partial(body, names, line, plane, r), out_shape=...  63.1 us
    pallas_call x1, Pallas kernels, on_device(): pl.pallas_call(functools.partial(finish, r), out_shape=(jax.ShapeDtypeStr...  2.36 us

profile of v4, /device:TPU:0, one launch (start us, length us, event | category | flops | bytes accessed | tf_op | source)
XLA Modules:
  0.0 66.3 jit_solution(7717667216799159259)
XLA Ops:
  0.7 63.1 %loop_block.1 = (bf16[1024,256]{1,0:T(8,128)(2,1)}, bf16[1024,256]{1,0:T(8,128)(2,1)}, f32[10,16,256]{2,1,0:T(8,128)}, f32[2,16,384]{2,1,0:T(8,128)}, f32[16,256]{1,0:T(8,128)}) custom-call(bf16[1024,256]{1,0:T(8,128)(2,1)} %bitcast.20, bf16[1024,256]{1,0:T(8,128)(2,1)} %bitcast.21, s32[1,20]{1,0:T(1,128)} %refs_2_.1, s32[1,20]{1,0:T(1,128)} %refs_3_.1, ...), custom_call_target="tpu_custom_call" | custom-call | tf_op jit(solution)/shard_map/loop_block/pallas_call | solution.py:637
  63.7 2.4 %finish.1 = (bf16[1024,256]{1,0:T(8,128)(2,1)}, bf16[1024,256]{1,0:T(8,128)(2,1)}, f32[16,256]{1,0:T(8,128)}, f32[16,256]{1,0:T(8,128)}, f32[16,256]{1,0:T(8,128...) custom-call(bf16[1024,256]{1,0:T(8,128)(2,1)} %get-tuple-element.33., ...), custom_call_target="tpu_custom_call" | custom-call | tf_op jit(solution)/shard_map/finish/pallas_call | solution.py:655

commit v5 on v4

--- a/solution.py
+++ b/solution.py
@@ -229,16 +229,20 @@
             return s["state"][rows, :]
         return jnp.where(wide(s["act"][rows, :]) > 0, cot[rows, :].astype(F32), 0.0)
 
+    def backward_down(t, i):
+        rows = pl.ds(pl.multiple_of(i * C, C), C)
+        b2t = back_renewed(t, rows).astype(BF).T
+        for c in range(4):
+            add(G, WD + c, t, dot(b2t, s["h"][t, c, rows, :]))
+
     def backward_hidden(t, i):
         rows = pl.ds(pl.multiple_of(i * C, C), C)
         br = back_renewed(t, rows)
         add(gs, slice(4, 5), t, jnp.sum(br, axis=0, keepdims=True))
         b2 = br.astype(BF)
-        b2t = b2.T
         n2t = s["n2"][t, rows, :].T
         dn2 = jnp.zeros((C, D), F32)
         for c in range(4):
-            add(G, WD + c, t, dot(b2t, s["h"][t, c, rows, :]))
             dp = s["d"][t, c, rows, :].astype(F32) * dot(b2, W(WD + c))
             add(gs, slice(5 + c, 6 + c), t, jnp.sum(dp, axis=0, keepdims=True))
             dp = dp.astype(BF)
@@ -266,10 +270,10 @@
                 ref[ahead, :] += value[QB:]
 
     def backward_late(t, i):
-        backward_scores(t, i, range(C // QB // 2, C // QB))
+        backward_scores(t, i, range(C // QB * 5 // 8, C // QB))
 
     def backward_early(t, i):
-        backward_scores(t, i, range(C // QB // 2))
+        backward_scores(t, i, range(C // QB * 5 // 8))
         rows = pl.ds(pl.multiple_of(i * C, C), C)
         own_keys = pl.ds(pl.multiple_of(i * C, C) + QB, C)
         n1t = s["n1"][t, rows, :].T
@@ -293,7 +297,7 @@
             ing[rows, :] = (s["bi"][rows, :] + 2.0 * bm).astype(BF)
 
     forward = (forward_mixed, forward_attention, forward_hidden)
-    return forward, (backward_hidden, backward_late, backward_early, backward_mixed)
+    return forward, (backward_down, backward_hidden, backward_late, backward_early, backward_mixed)
 
 
 def body(names, line, plane, r, *refs):
@@ -381,7 +385,7 @@
     C = S if rp == r else 256
     forward, backward = block(s, W, C)
     forward_mixed, forward_attention, forward_hidden = forward
-    backward_hidden, backward_late, backward_early, backward_mixed = backward
+    backward_down, backward_hidden, backward_late, backward_early, backward_mixed = backward
 
     def chunks(t, *steps):
         def one(i):
@@ -504,27 +508,38 @@
         return ref
 
     left(to_a, to_b, to_c, to_b2, to_c2, share_a, share_b, share_c)
-    gb_u, gb_d, gb_q = gb.at[pl.ds(0, 6)], gb.at[pl.ds(6, 4)], s["gq"]
-    res_q, res_u, res_d = s["resq"], res.at[pl.ds(0, 6)], res.at[pl.ds(6, 4)]
-
+    gb_u, gb_d, gb_q = gb.at[pl.ds(0, 4)], gb.at[pl.ds(4, 4)], s["gq"]
+    res_q, res_u, res_d = s["resq"], res.at[pl.ds(0, 4)], res.at[pl.ds(4, 4)]
+
+    def first_hop(k, ref, inbox):
+        return across_plane(k, inbox, lambda p: kept(ref).at[:, :, p], lambda i: inbox.at[i - 1])
+
+    def second_hop(k, sums, inbox):
+        return along_line(k, inbox, lambda a: sums.at[:, a], lambda i: inbox.at[i - 1])
+
+    chunks(0, backward_down)
+    stage(4, WD, WD + 1, WD + 2, WD + 3)
+    swap_d = swap(8, gb_d, s["ind"])
     chunks(0, backward_hidden)
-    stage(6, WD, WD + 1, WD + 2, WD + 3)
-    swap_d = swap(8, gb_d, s["ind"])
-    stage(0, WO, WU, WU + 1, WU + 2, WU + 3)
-    gb[5] = jnp.zeros(gb.shape[1:], BF)
+    stage(0, WU, WU + 1, WU + 2, WU + 3)
     swap_u = swap(9, gb_u, s["inu"])
+    add_swapped(swap_d, gb_d, s["ind"])
+    from_d = first_hop(10, gb_d, s["in1d"])
     no_keys_ahead(s)
-    chunks(0, backward_late)
-    add_swapped(swap_d, gb_d, s["ind"])
-    from_d = along_line(10, s["in1d"], lambda a: kept(gb_d).at[:, a], lambda i: s["in1d"].at[i - 1])
+    if S == C:
+        chunks(0, backward_late)
     add_swapped(swap_u, gb_u, s["inu"])
-    from_u = across_plane(11, s["in1u"], lambda p: kept(gb_u).at[:, :, p], lambda i: s["in1u"].at[i - 1])
-    chunks(0, backward_early)
+    from_u = first_hop(11, gb_u, s["in1u"])
+    if S == C:
+        chunks(0, backward_early)
+    else:
+        chunks(0, backward_late, backward_early)
     gb_q[0, :, :, :, 0:D] = blocks(WQ)
     gb_q[1, :, :, :, 0:D] = blocks(WK)
-    value_blocks = blocks(WV)
-    for c in range(2):
-        gb_q[c, :, :, :, pl.ds(D, 128)] = value_blocks[:, :, :, 128 * c : 128 * (c + 1)]
+    for at, i in ((D, WV), (D + 128, WO)):
+        halves = blocks(i)
+        for c in range(2):
+            gb_q[c, :, :, :, pl.ds(at, 128)] = halves[:, :, :, 128 * c : 128 * (c + 1)]
     swap_q = swap(15, gb_q, s["inq"])
     chunks(0, backward_mixed)
     store_ing.start()
@@ -532,27 +547,30 @@
     vectors[...] = gs[...].astype(BF)
     near = [{"dp": other, "wide": x.chip(x.a, x.across(i))["wide"]} for other in (core, 1 - core) for i in range(plane)]
     from_v = start_all(23, s["inv"], [(vectors, s["inv"].at[i], device) for i, device in enumerate(near[1:])])
+    arrived(from_d)
+    sumd = summed(s["sumd"], kept(gb_d)[:, :, x.p], s["in1d"])
+    from_d2 = second_hop(14, sumd, s["in2d"])
     add_swapped(swap_q, gb_q, s["inq"])
-    from_q = straight(16, gb_q, s["intq"])
-    arrived(from_d)
-    sumd = summed(s["sumd"], kept(gb_d)[:, x.a], s["in1d"])
-    from_d2 = across_plane(14, s["in2d"], lambda p: sumd.at[:, p], lambda i: s["in2d"].at[i - 1])
+    from_q = first_hop(16, gb_q, s["in1q"])
     arrived(from_u)
     sumu = summed(s["sumu"], kept(gb_u)[:, :, x.p], s["in1u"])
-    from_u2 = along_line(17, s["in2u"], lambda a: sumu.at[:, a], lambda i: s["in2u"].at[i - 1])
+    from_u2 = second_hop(17, sumu, s["in2u"])
     arrived(from_v)
     sumv = summed(s["sumv"], vectors[...], s["inv"])
     from_v2 = along_line(24, s["in2v"], lambda _: sumv, lambda i: s["in2v"].at[i - 1])
+    arrived(from_q)
+    sumq = summed(s["sumq"], kept(gb_q)[:, :, x.p], s["in1q"])
+    from_q2 = second_hop(13, sumq, s["in2q"])
     arrived(from_d2)
-    done_d = finished(18, res_d, total(sumd[:, x.p], s["in2d"]))
+    done_d = finished(18, res_d, total(sumd[:, x.a], s["in2d"]))
     arrived(from_u2)
     done_u = finished(20, res_u, total(sumu[:, x.a], s["in2u"]))
-    arrived(from_q)
-    done_q = finished(21, res_q, total(kept(gb_q)[:, x.a, x.p], s["intq"]))
     arrived(from_v2)
     s["vec"][...] = total(sumv[...], s["in2v"])
+    arrived(from_q2)
+    done_q = finished(21, res_q, total(sumq[:, x.a], s["in2q"]))
     arrived(done_d, done_u, done_q)
-    left(swap_d, swap_u, swap_q, from_d, from_d2, from_u, from_u2, from_q, from_v, from_v2)
+    left(swap_d, swap_u, swap_q, from_d, from_d2, from_u, from_u2, from_q, from_q2, from_v, from_v2)
     left(done_d, done_u, done_q)
     store_out.wait()
     store_ing.wait()
@@ -566,13 +584,14 @@
         large=pltpu.SemaphoreType.DMA((4,)), tile=V((16, D), F32), small=V((16, D), F32),
         wb=V((SLABS, line, plane, rp, D), BF),
         G=V((SLABS, D, D), F32), gs=V((16, D), F32),
-        gq=V((2, line, plane, rp, D + 128), BF), inq=V((1, line, plane, rp, D + 128), BF),
-        intq=V((n - 1, 1, rp, D + 128), BF), size=V((3, n, rp, D), BF),
+        gq=V((2, line, plane, rp, 2 * D), BF), inq=V((1, line, plane, rp, 2 * D), BF),
+        in1q=V((plane - 1, 1, line, rp, 2 * D), BF), in2q=V((line - 1, 1, rp, 2 * D), BF), sumq=V((1, line, rp, 2 * D), BF),
+        size=V((3, n, rp, D), BF),
         vectors=V((16, D), BF), inv=V((2 * plane - 1, 16, D), BF), sumv=V((16, D), BF), in2v=V((line - 1, 16, D), BF),
-        inu=V((3, line, plane, rp, D), BF), in1u=V((plane - 1, 3, line, rp, D), BF),
-        in2u=V((line - 1, 3, rp, D), BF), sumu=V((3, line, rp, D), BF),
-        ind=V((2, line, plane, rp, D), BF), in1d=V((line - 1, 2, plane, rp, D), BF),
-        in2d=V((plane - 1, 2, rp, D), BF), sumd=V((2, plane, rp, D), BF),
+        inu=V((2, line, plane, rp, D), BF), in1u=V((plane - 1, 2, line, rp, D), BF),
+        in2u=V((line - 1, 2, rp, D), BF), sumu=V((2, line, rp, D), BF),
+        ind=V((2, line, plane, rp, D), BF), in1d=V((plane - 1, 2, line, rp, D), BF),
+        in2d=V((line - 1, 2, rp, D), BF), sumd=V((2, line, rp, D), BF),
         mask=V((nb, QB, 2 * QB), F32), act=V((S, 128), F32), state=V((S, D), F32), mixed=V((S, D), F32),
         z1=V((2, S, D), F32), r1=V((2, S, 128), F32), n1=V((2, S, D), BF),
         z2=V((2, S, D), F32), r2=V((2, S, 128), F32), n2=V((2, S, D), BF),
@@ -585,7 +604,7 @@
     if D // n != rp:
         shapes["wf"] = V((SLABS, D, D), BF)
     else:
-        shapes["gb"] = V((10, line, plane, rp, D), BF)
+        shapes["gb"] = V((8, line, plane, rp, D), BF)
     shapes["send"] = pltpu.SemaphoreType.DMA((25,))
     shapes["recv"] = pltpu.SemaphoreType.DMA((25,))
     return shapes
@@ -600,11 +619,12 @@
     gq[...] = resq[0, 0:r, 0:D]
     gk[...] = resq[1, 0:r, 0:D]
     for c in range(2):
-        gv[:, 128 * c : 128 * (c + 1)] = resq[c, 0:r, D:]
-    go[...] = res[0, 0:r, :]
+        half = slice(128 * c, 128 * (c + 1))
+        gv[:, half] = resq[c, 0:r, D : D + 128]
+        go[:, half] = resq[c, 0:r, D + 128 :]
     for c in range(4):
-        gu[:, c * D : (c + 1) * D] = res[1 + c, 0:r, :]
-        gd[:, c * D : (c + 1) * D] = res[6 + c, 0:r, :]
+        gu[:, c * D : (c + 1) * D] = res[c, 0:r, :]
+        gd[:, c * D : (c + 1) * D] = res[4 + c, 0:r, :]
     tile = vec[...]
     own = pltpu.roll(tile, lax.rem(D - me * r, D), axis=1)
     for i, ref in enumerate((gg1, gs1, gg2, gs2, gbd)):
@@ -639,8 +659,8 @@
         out_shape=(
             jax.ShapeDtypeStruct((S, D), BF),
             jax.ShapeDtypeStruct((S, D), BF),
-            jax.ShapeDtypeStruct((10, rp, D), F32),
-            jax.ShapeDtypeStruct((2, rp, D + 128), F32),
+            jax.ShapeDtypeStruct((8, rp, D), F32),
+            jax.ShapeDtypeStruct((2, rp, 2 * D), F32),
             jax.ShapeDtypeStruct((16, D), F32),
         ),
         in_specs=[hbm] * len(inputs),

time: 66.4 us -> 65.6 us (0.988)
  Pallas kernels: 65.4 us -> 64.6 us
    pallas_call x1, Pallas kernels: 63.1 us -> 62.2 us  [on_device(): pl.pallas_call(functools.partial(body, names, line, plane, r), out_shape=...]
where the time goes in v5:
time: 65.6 us; the launch traced here: 65.4 us
  Pallas kernels  64.6 us (98%)
  between operations  0.84 us (1%)
    pallas_call x1, Pallas kernels, on_device(): pl.pallas_call(functools.partial(body, names, line, plane, r), out_shape=...  62.2 us
    pallas_call x1, Pallas kernels, on_device(): pl.pallas_call(functools.partial(finish, r), out_shape=(jax.ShapeDtypeStr...  2.36 us

profile of v5, /device:TPU:0, one launch (start us, length us, event | category | flops | bytes accessed | tf_op | source)
XLA Modules:
  0.0 65.4 jit_solution(13603448199610258632)
XLA Ops:
  0.7 62.2 %loop_block.1 = (bf16[1024,256]{1,0:T(8,128)(2,1)}, bf16[1024,256]{1,0:T(8,128)(2,1)}, f32[8,16,256]{2,1,0:T(8,128)}, f32[2,16,512]{2,1,0:T(8,128)}, f32[16,256]{1,0:T(8,128)}) custom-call(bf16[1024,256]{1,0:T(8,128)(2,1)} %bitcast.20, bf16[1024,256]{1,0:T(8,128)(2,1)} %bitcast.21, s32[1,20]{1,0:T(1,128)} %refs_2_.1, s32[1,20]{1,0:T(1,128)} %refs_3_.1, ...), custom_call_target="tpu_custom_call" | custom-call | tf_op jit(solution)/shard_map/loop_block/pallas_call | solution.py:657
  62.9 2.4 %finish.1 = (bf16[1024,256]{1,0:T(8,128)(2,1)}, bf16[1024,256]{1,0:T(8,128)(2,1)}, f32[16,256]{1,0:T(8,128)}, f32[16,256]{1,0:T(8,128)}, f32[16,256]{1,0:T(8,128...) custom-call(bf16[1024,256]{1,0:T(8,128)(2,1)} %get-tuple-element.33., ...), custom_call_target="tpu_custom_call" | custom-call | tf_op jit(solution)/shard_map/finish/pallas_call | solution.py:675

commit v6 on v5

--- a/solution.py
+++ b/solution.py
@@ -413,8 +413,8 @@
     def along_line(k, size, ref, inbox):
         return start_all(k, size, [(ref(x.along(i)), inbox(i), x.chip(x.along(i), x.p)) for i in range(1, line)])
 
-    def across_plane(k, size, ref, inbox):
-        return start_all(k, size, [(ref(x.across(i)), inbox(i), x.chip(x.a, x.across(i))) for i in range(1, plane)])
+    def across_plane(k, size, ref, inbox, steps=range(1, plane)):
+        return start_all(k, size, [(ref(x.across(i)), inbox(i), x.chip(x.a, x.across(i))) for i in steps])
 
     def to_sibling(k, size, src, dst):
         return start_all(k, size, [(src, dst, x.sibling())])
@@ -434,9 +434,10 @@
     to_a = start_all(2, bytes_of(GROUP_A, n - 1), [(own_a, own_a, device) for device in everyone])
     arrived(to_b)
     line_b, line_c = (mine(group).at[:, :, x.p] for group in (GROUP_B, GROUP_C))
-    to_b2 = across_plane(3, bytes_of(GROUP_B, line * (plane - 1)), lambda _: line_b, lambda _: line_b)
+    nearest_last = range(plane - 1, 0, -1)
+    to_b2 = across_plane(3, bytes_of(GROUP_B, line * (plane - 1)), lambda _: line_b, lambda _: line_b, nearest_last)
     arrived(to_c)
-    to_c2 = across_plane(4, bytes_of(GROUP_C, line * (plane - 1)), lambda _: line_c, lambda _: line_c)
+    to_c2 = across_plane(4, bytes_of(GROUP_C, line * (plane - 1)), lambda _: line_c, lambda _: line_c, nearest_last)
     arrived(to_a)
     share_a = share(5, GROUP_A)
     arrived(share_a)

time: 65.6 us -> 65.6 us (level)
  no operation moved by 1% of the time
where the time goes in v6:
time: 65.6 us; the launch traced here: 65.4 us
  Pallas kernels  64.6 us (98%)
  between operations  0.84 us (1%)
    pallas_call x1, Pallas kernels, on_device(): pl.pallas_call(functools.partial(body, names, line, plane, r), out_shape=...  62.2 us
    pallas_call x1, Pallas kernels, on_device(): pl.pallas_call(functools.partial(finish, r), out_shape=(jax.ShapeDtypeStr...  2.36 us

profile of v6, /device:TPU:0, one launch (start us, length us, event | category | flops | bytes accessed | tf_op | source)
XLA Modules:
  0.0 65.4 jit_solution(5224967668122154888)
XLA Ops:
  0.7 62.2 %loop_block.1 = (bf16[1024,256]{1,0:T(8,128)(2,1)}, bf16[1024,256]{1,0:T(8,128)(2,1)}, f32[8,16,256]{2,1,0:T(8,128)}, f32[2,16,512]{2,1,0:T(8,128)}, f32[16,256]{1,0:T(8,128)}) custom-call(bf16[1024,256]{1,0:T(8,128)(2,1)} %bitcast.20, bf16[1024,256]{1,0:T(8,128)(2,1)} %bitcast.21, s32[1,20]{1,0:T(1,128)} %refs_2_.1, s32[1,20]{1,0:T(1,128)} %refs_3_.1, ...), custom_call_target="tpu_custom_call" | custom-call | tf_op jit(solution)/shard_map/loop_block/pallas_call | solution.py:658
  62.9 2.4 %finish.1 = (bf16[1024,256]{1,0:T(8,128)(2,1)}, bf16[1024,256]{1,0:T(8,128)(2,1)}, f32[16,256]{1,0:T(8,128)}, f32[16,256]{1,0:T(8,128)}, f32[16,256]{1,0:T(8,128...) custom-call(bf16[1024,256]{1,0:T(8,128)(2,1)} %get-tuple-element.33., ...), custom_call_target="tpu_custom_call" | custom-call | tf_op jit(solution)/shard_map/finish/pallas_call | solution.py:676
